TPU v7x, 32 devices: a whole 2x2x4 slice. The times are simulated.
32 devices in a mesh: bank: 4 (over y, core), gal: 8 (over z, x).
Axes of the slice: x: 2, y: 2, z: 4, core: 2. Of those that a mesh axis runs over, the one named last changes fastest.
Arguments:
- querybank: bfloat16 [4096, 512], P(('bank', 'gal')), may hold values from -80 to 80
- gallery: bfloat16 [32768, 512], P('gal'), may hold values from -80 to 80
- test_queries: bfloat16 [512, 512], P(('bank', 'gal')), may hold values from -80 to 80
Outputs:
- retrieval: float32 [512, 8, 4096], P(None, 'gal', 'bank')
All inputs are finite; a program needn't handle non-finite values.
Results may differ from a plain program's by a relative error of at most 0.0017.
Values may be sent and summed in bfloat16 or wider, within the bound.
No kernel may reach another device: no remote copies, remote signals or barrier semaphores. Data moves between devices by JAX's collectives and lax.ppermute only.
A program may use at most 64 MiB of HBM per device.

v0:
```python
import jax
import jax.numpy as jnp
from jax import lax
from jax.sharding import PartitionSpec as P

inverse_temp = 20.0
epsilon = 1e-06


def unit_rows(values):
    wide = values.astype(jnp.float32)
    return (wide * lax.rsqrt(jnp.sum(wide * wide, axis=-1, keepdims=True) + epsilon)).astype(
        jnp.bfloat16
    )


def exp_sums(piece, clips_t):
    rows = piece.shape[0]
    blocks = piece.reshape(rows // 512, 512, piece.shape[1])

    def one_block(total, block):
        sims = jnp.dot(block, clips_t, preferred_element_type=jnp.float32)
        return (total + jnp.sum(jnp.exp(inverse_temp * sims), axis=0), None)

    start_total = jnp.zeros((clips_t.shape[1],), jnp.float32)
    total, unused = lax.scan(one_block, start_total, blocks)
    return total


def local(querybank, gallery, test_queries):
    clips_t = unit_rows(gallery).T
    captions = unit_rows(querybank)
    tests = unit_rows(test_queries)
    groups = lax.axis_size("bank")
    count = captions.shape[0] * lax.axis_size("gal") * groups
    share = clips_t.shape[1] // groups
    partial_sums = exp_sums(lax.all_gather(captions, "gal", axis=0, tiled=True), clips_t)
    totals = lax.psum(partial_sums, "bank")
    mine = lax.dynamic_slice_in_dim(totals, lax.axis_index("bank") * share, share, 0)
    every_test = lax.all_gather(tests, ("bank", "gal"), axis=0, tiled=True)
    columns = lax.dynamic_slice_in_dim(clips_t, lax.axis_index("bank") * share, share, 1)
    sims = jnp.dot(every_test, columns, preferred_element_type=jnp.float32)
    result = inverse_temp * sims - jnp.log(mine / count)[None, :]
    return result[:, None, :]


def solution(mesh):
    placed = (P(("bank", "gal"), None), P("gal", None), P(("bank", "gal"), None))
    return jax.shard_map(
        local, mesh=mesh, in_specs=placed, out_specs=P(None, "gal", "bank"), check_vma=False
    )
```

profile of v0, /device:TPU:0, one launch (start us, length us, event | category | flops | bytes accessed | tf_op | source)
XLA Modules:
  0.0 132.7 jit_solution(12711882285434026488)
XLA Ops:
  6.5 0.0 all-gather.2.cloned.1.call-start
  6.5 1.0 fusion.6
  7.6 1.7 %fusion.7 = bf16[128,512]{1,0:T(8,128)(2,1)} fusion(bf16[128,512]{1,0:T(8,128)(2,1)} %param.5, f32[128]{0:T(128)S(1)} %add_rsqrt_fusion.1), kind=kLoop, calls=%fused_computation.14 | loop fusion | flops 196608 | bytes 262656 | tf_op jit(solution)/shard_map/convert_element_type | solution.py:12
  9.2 0.0 all-gather.2.cloned.1.call-update
  9.3 6.4 %copy.4 = bf16[4096,512]{0,1:T(8,128)(2,1)} copy(bf16[4096,512]{1,0:T(8,128)(2,1)} %param.6) | data formatting | bytes 8388608 | tf_op args[1]
  15.7 0.0 copy-start.1
  15.7 3.1 %fusion.3 = f32[4096]{0:T(1024)S(1)} fusion(bf16[4096,512]{0,1:T(8,128)(2,1)} %copy.4), kind=kLoop, calls=%fused_computation.7 | loop fusion | flops 6287360 | bytes 4210688 | tf_op jit(solution)/shard_map/reduce_sum | solution.py:12
  18.8 0.0 copy-done.1
  18.8 0.1 fusion.8
  18.9 0.1 fusion.9
  19.0 73.3 %all_gather.6 = bf16[512,512]{1,0:T(8,128)(2,1)S(1)} all-gather(bf16[16,512]{1,0:T(8,128)(2,1)S(1)} %fusion.9), channel_id=1, replica_groups=mesh['bank'=4,'gal'=8] {'bank','gal'}, dimensions={0}, use_global_device_ids=true | all-gather | bytes 540672 | tf_op jit(solution)/shard_map/all_gather | solution.py:40
  92.3 0.0 copy-start
  92.3 5.4 %fusion.13 = bf16[512,4096]{1,0:T(8,128)(2,1)} fusion(f32[4096]{0:T(1024)S(1)} %add_rsqrt_fusion, bf16[4096,512]{0,1:T(8,128)(2,1)} %copy.4), kind=kLoop, calls=%fused_computation.24 | loop fusion | flops 6291456 | bytes 8404992 | tf_op jit(solution)/shard_map/transpose | solution.py:31
  97.7 0.0 copy-done
  97.7 2.8 %fusion.4 = bf16[4096,512]{0,1:T(8,128)(2,1)} fusion(bf16[4096,512]{0,1:T(8,128)(2,1)S(1)} %copy-done, f32[4096]{0:T(1024)S(1)} %add_rsqrt_fusion), kind=kLoop, calls=%fused_computation.8 | loop fusion | flops 6291456 | bytes 8404992 | tf_op jit(solution)/shard_map/convert_element_type | solution.py:12
  100.5 0.0 all-gather.2.cloned.1.call-done
  100.5 9.6 %while.11 = (s32[]{:T(128)}, f32[4096]{0:T(1024)S(1)}, bf16[2,512,512]{2,1,0:T(8,128)(2,1)}, bf16[512,4096]{1,0:T(8,128)(2,1)}, s32[]{:T(128)}, /*index=5*/s32[]{:T(128)}) while((s32[]{:T(128)}, f32[4096]{0:T(1024)S(1)}, bf16[2,512,512]{2,1,0:T(8,128)(2,1)}, bf16[512,4096]{1,0:T(8,128)(2,1)}, s32[]{:T(128)}, ...), condition=%wide.region_5.6_spmd.clone, body=%wide.region_3.5_spmd.clone.sunk | while | flops 2151682048 | bytes 4784719 | solution.py:26
  100.5 4.8 %exponential_reduce_fusion.2 = f32[4096]{0:T(1024)S(1)} fusion(bf16[512,4096]{1,0:T(8,128)(2,1)} %get-tuple-element.91, bf16[2,512,512]{2,1,0:T(8,128)(2,1)} %get-tuple-element.90, s32[]{:T(128)} %get-tuple-element.82), kind=kOutput, calls=%fused_computation.clone.1 | convolution fusion | flops 2151673856 | bytes 4735488 | tf_op jit(solution)/shard_map/while/body/eval_jaxpr/dot_general | solution.py:22
  105.3 4.8 %exponential_reduce_fusion.2 = f32[4096]{0:T(1024)S(1)} fusion(bf16[512,4096]{1,0:T(8,128)(2,1)} %get-tuple-element.91, bf16[2,512,512]{2,1,0:T(8,128)(2,1)} %get-tuple-element.90, s32[]{:T(128)} %get-tuple-element.82), kind=kOutput, calls=%fused_computation.clone.1 | convolution fusion | flops 2151673856 | bytes 4735488 | tf_op jit(solution)/shard_map/while/body/eval_jaxpr/dot_general | solution.py:22
  110.1 10.3 %psum.7 = f32[4096]{0:T(1024)S(1)} all-reduce(f32[4096]{0:T(1024)S(1)} %get-tuple-element.27), channel_id=1, replica_groups=mesh['bank'=4,'gal'=8] {'bank'}, use_global_device_ids=true, to_apply=%region_6.7 | all-reduce | flops 4096 | bytes 32768 | tf_op jit(solution)/shard_map/psum | solution.py:38
  120.4 1.9 %subtract_bitcast_fusion = f32[512,1,1024]{2,0,1:T(8,128)S(1)} fusion(bf16[512,512]{1,0:T(8,128)(2,1)S(1)} %all_gather.6, f32[1024]{0:T(1024)S(1)} %multiply_log_fusion, bf16[4096,512]{0,1:T(8,128)(2,1)} %fusion.4, s32[]{:T(128)S(6)} %select_n.4), kind=kOutput, calls=%fused_computation.9 | convolution fusion | flops 537919488 | bytes 3674116 | tf_op jit(solution)/shard_map/dot_general | solution.py:42
  122.3 3.5 %copy.5 = f32[512,1,1024]{2,1,0:T(1,128)} copy(f32[512,1,1024]{2,0,1:T(8,128)S(1)} %subtract_bitcast_fusion) | data formatting | bytes 4194304 | tf_op jit(solution)/shard_map/broadcast_in_dim | solution.py:44
  (7 shorter events, 0.0 us)
Async XLA Ops:
  6.5 93.9 %all-gather.2.cloned.1.call-start = ((), (), s32[]{:S(2)}) async-start(), calls=%async_computation | async-start | bytes 1179648 | tf_op jit(solution)/shard_map/all_gather | solution.py:37
  15.7 3.1 %copy-start.1 = (bf16[16,512]{1,0:T(8,128)(2,1)S(1)}, bf16[16,512]{1,0:T(8,128)(2,1)}, u32[]{:S(2)}) copy-start(bf16[16,512]{1,0:T(8,128)(2,1)} %param.7) | copy-start | bytes 49156
  92.3 5.4 %copy-start = (bf16[4096,512]{0,1:T(8,128)(2,1)S(1)}, bf16[4096,512]{0,1:T(8,128)(2,1)}, u32[]{:S(2)}) copy-start(bf16[4096,512]{0,1:T(8,128)(2,1)} %copy.4) | copy-start | bytes 12582916
Sparse Core Ops, SparseCore 0:
  9.5 43.3 all-gather.1
where the time goes:
time: 133 us
  blocking collectives  83.6 us (63%)
  other arithmetic  14.2 us (11%)
  between operations  13.5 us (10%)
  matrix products  11.5 us (9%)
  local copies, waits for them, and re-layouts  9.9 us (7%)
    all_gather x1, blocking collectives, local(): every_test = lax.all_gather(tests, ('bank', 'gal'), axis=0, tiled=True)  73.3 us
    psum x1, blocking collectives, local(): totals = lax.psum(partial_sums, 'bank')  10.3 us
    dot_general x2, matrix products, one_block(): sims = jnp.dot(block, clips_t, preferred_element_type=jnp.float32)  9.53 us
    unnamed x5, local copies, waits for them, and re-layouts  6.43 us
    transpose x1, other arithmetic, local(): clips_t = unit_rows(gallery).T  5.4 us
    convert_element_type x3, other arithmetic, unit_rows(): (wide * lax.rsqrt(jnp.sum(wide * wide, axis=-1, keepdims=True) + epsilon)...  4.54 us
    reduce_sum x3, other arithmetic, unit_rows(): jnp.sum(wide * wide, axis=-1, keepdims=True) + epsilon  4.21 us
    broadcast_in_dim x1, local copies, waits for them, and re-layouts, local(): return result[:, None, :]  3.48 us
  transfers between devices with their start and end apart: 1, of which 0 were waited for; matrix products, arithmetic and copies ran while one was open for 13% of the time, Pallas kernels for 0%

commit v1 on v0

v1 whole, which is shorter than its diff:
```python
import functools

import jax
import jax.numpy as jnp
from jax import lax
from jax.experimental import pallas as pl
from jax.experimental.pallas import tpu as pltpu
from jax.sharding import PartitionSpec as P

inverse_temp = 20.0
epsilon = 1e-06
log2_e = 1.4426950408889634
vmem_bytes = 32 * 1024 * 1024


def unit_rows(values):
    wide = values.astype(jnp.float32)
    return (wide * lax.rsqrt(jnp.sum(wide * wide, axis=-1, keepdims=True) + epsilon)).astype(
        jnp.bfloat16
    )


def exp_sums(captions, clips):
    sims = lax.dot_general(
        captions, clips, (((1,), (1,)), ((), ())), preferred_element_type=jnp.float32
    )
    grown = jnp.exp2(sims * (inverse_temp * log2_e))
    return jnp.sum(grown.reshape(grown.shape[0] // 8, 8, grown.shape[1]), axis=0)


def params():
    return pltpu.CompilerParams(vmem_limit_bytes=vmem_bytes)


def prepare(captions, tests):
    rows, more, width = captions.shape[0], tests.shape[0], captions.shape[1]

    def kernel(captions_ref, tests_ref, out_ref):
        out_ref[:rows, :] = unit_rows(captions_ref[...])
        out_ref[rows:, :] = unit_rows(tests_ref[...])

    return pl.pallas_call(
        kernel,
        out_shape=jax.ShapeDtypeStruct((rows + more, width), jnp.bfloat16),
        compiler_params=params(),
        name="prepare",
    )(captions, tests)


def first_sums(bank, gallery, payload, rows, share):
    clips, width = gallery.shape
    block = share // 2

    def kernel(bank_ref, gallery_ref, payload_ref, unit_ref, sums_ref):
        unit = unit_rows(gallery_ref[...])
        unit_ref[...] = unit
        sums_ref[...] = exp_sums(payload_ref[...], unit)

    return pl.pallas_call(
        kernel,
        grid_spec=pltpu.PrefetchScalarGridSpec(
            num_scalar_prefetch=1,
            grid=(clips // block,),
            in_specs=[
                pl.BlockSpec((block, width), lambda j, b: (((j // 2) ^ b[0]) * 2 + j % 2, 0)),
                pl.BlockSpec((rows, width), lambda j, b: (0, 0)),
            ],
            out_specs=[
                pl.BlockSpec((block, width), lambda j, b: (j, 0)),
                pl.BlockSpec((8, block), lambda j, b: (0, j)),
            ],
        ),
        out_shape=[
            jax.ShapeDtypeStruct((clips, width), jnp.bfloat16),
            jax.ShapeDtypeStruct((8, clips), jnp.float32),
        ],
        cost_estimate=pl.CostEstimate(
            flops=2 * rows * clips * width, bytes_accessed=4 * clips * width, transcendentals=0
        ),
        compiler_params=params(),
        name="first_sums",
    )(bank, gallery, payload)


def more_sums(unit, payloads, sums, rows, share):
    clips, width = unit.shape
    block = share // 2
    count = len(payloads)

    def kernel(unit_ref, *refs):
        total = refs[count][...]
        for ref in refs[:count]:
            total = total + exp_sums(ref[...], unit_ref[...])
        refs[count + 1][...] = total

    return pl.pallas_call(
        kernel,
        grid=(clips // block,),
        in_specs=[pl.BlockSpec((block, width), lambda j: (j, 0))]
        + [pl.BlockSpec((rows, width), lambda j: (0, 0))] * count
        + [pl.BlockSpec((8, block), lambda j: (0, j))],
        out_specs=pl.BlockSpec((8, block), lambda j: (0, j)),
        out_shape=jax.ShapeDtypeStruct((8, clips), jnp.float32),
        cost_estimate=pl.CostEstimate(
            flops=2 * rows * clips * width * count, bytes_accessed=2 * clips * width, transcendentals=0
        ),
        compiler_params=params(),
        name="more_sums",
    )(unit, *payloads, sums)


def last_sums(gal, unit, payloads, sums, every, rows, share):
    clips, width = unit.shape
    count, n = len(payloads), len(every)
    more = every[0].shape[0] - rows

    def kernel(gal_ref, unit_ref, *refs):
        step = pl.program_id(0)
        keep_ref, send_ref, tests_ref = refs[count + 1 + n :]
        total = refs[count][...]
        for ref in refs[:count]:
            total = total + exp_sums(ref[...], unit_ref[...])
        total = jnp.sum(total, axis=0, keepdims=True)

        @pl.when(step % 2 == 0)
        def even():
            keep_ref[pl.ds(step // 2, 1), :] = total

        @pl.when(step % 2 == 1)
        def odd():
            send_ref[pl.ds(step // 2, 1), :] = total

        @pl.when(step == 0)
        def tests():
            for mask in range(n):
                place = pl.multiple_of((gal_ref[0] ^ mask) * more, more)
                tests_ref[pl.ds(place, more), :] = refs[count + 1 + mask][...]

    half = clips // share // 2
    return pl.pallas_call(
        kernel,
        grid_spec=pltpu.PrefetchScalarGridSpec(
            num_scalar_prefetch=1,
            grid=(clips // share,),
            in_specs=[pl.BlockSpec((share, width), lambda j, g: (j, 0))]
            + [pl.BlockSpec((rows, width), lambda j, g: (0, 0))] * count
            + [pl.BlockSpec((8, share), lambda j, g: (0, j))]
            + [pl.BlockSpec((more, width), lambda j, g: (rows // more, 0))] * n,
            out_specs=[
                pl.BlockSpec((half, share), lambda j, g: (0, 0)),
                pl.BlockSpec((half, share), lambda j, g: (0, 0)),
                pl.BlockSpec((n * more, width), lambda j, g: (0, 0)),
            ],
        ),
        out_shape=[
            jax.ShapeDtypeStruct((half, share), jnp.float32),
            jax.ShapeDtypeStruct((half, share), jnp.float32),
            jax.ShapeDtypeStruct((n * more, width), jnp.bfloat16),
        ],
        cost_estimate=pl.CostEstimate(
            flops=2 * rows * clips * width * count, bytes_accessed=2 * clips * width, transcendentals=0
        ),
        compiler_params=params(),
        name="last_sums",
    )(gal, unit, *payloads, sums, *every)


def scores(bank, unit, tests, parts, total_count, share):
    width = unit.shape[1]
    rows = tests[0].shape[0]
    lanes = 128
    per_row = share // lanes
    n = len(tests)

    def kernel(bank_ref, unit_ref, *refs):
        out_ref = refs[-1]
        step = pl.program_id(0)
        norm = refs[n][0:1, :] + refs[n + 1][0:1, :] + refs[n + 2][...]
        shift = jnp.log(norm / total_count)
        for which in range(n):

            @pl.when(step == which)
            def one(which=which):
                sims = lax.dot_general(
                    refs[which][...],
                    unit_ref[...],
                    (((1,), (1,)), ((), ())),
                    preferred_element_type=jnp.float32,
                )
                values = inverse_temp * sims - shift
                for k in range(per_row):
                    out_ref[pl.ds(k, rows, stride=per_row), :] = values[:, k * lanes : (k + 1) * lanes]

    return pl.pallas_call(
        kernel,
        grid_spec=pltpu.PrefetchScalarGridSpec(
            num_scalar_prefetch=1,
            grid=(n,),
            in_specs=[pl.BlockSpec((share, width), lambda i, b: (0, 0))]
            + [pl.BlockSpec((rows, width), lambda i, b: (0, 0))] * n
            + [pl.BlockSpec(part.shape, lambda i, b: (0, 0)) for part in parts],
            out_specs=pl.BlockSpec((rows * per_row, lanes), lambda i, b: (i ^ b[0], 0)),
        ),
        out_shape=jax.ShapeDtypeStruct((n * rows * per_row, lanes), jnp.float32),
        cost_estimate=pl.CostEstimate(
            flops=2 * n * rows * share * width, bytes_accessed=4 * n * rows * share, transcendentals=0
        ),
        compiler_params=params(),
        name="scores",
    )(bank, unit, *tests, *parts)


def swap(values, axis, mask):
    size = lax.axis_size(axis)
    return lax.ppermute(values, axis, [(i, i ^ mask) for i in range(size)])


def local(querybank, gallery, test_queries):
    groups, shards = lax.axis_size("bank"), lax.axis_size("gal")
    rows = querybank.shape[0]
    share = gallery.shape[0] // groups
    bank = lax.axis_index("bank").astype(jnp.int32)[None]
    gal = lax.axis_index("gal").astype(jnp.int32)[None]

    payload = prepare(querybank, test_queries)
    low = shards // 4
    got = {0: payload}
    for high in (2, 3, 1):
        got[high * low] = swap(payload, "gal", high * low)
    for mask in range(1, low):
        got[mask] = swap(payload, "gal", mask)
        got[low + mask] = swap(payload, "gal", low + mask)
    for high in (2, 3):
        for mask in range(1, low):
            got[high * low + mask] = swap(got[high * low], "gal", mask)

    unit, sums = first_sums(bank, gallery, payload, rows, share)
    sums = more_sums(unit, [got[m] for m in range(1, 2 * low)], sums, rows, share)
    sums = more_sums(unit, [got[2 * low], got[3 * low]], sums, rows, share)
    last = [got[h * low + m] for h in (2, 3) for m in range(1, low)]
    keep, send, tests = last_sums(
        gal, unit, last, sums, [got[m] for m in range(shards)], rows, share
    )

    tests_y = swap(tests, "bank", 2)
    tests_core = swap(tests, "bank", 1)
    received = swap(send, "bank", 1)
    far = swap(keep[1:] + received[1:], "bank", 2)
    tests_both = swap(tests_y, "bank", 1)
    result = scores(
        bank,
        unit,
        [tests, tests_core, tests_y, tests_both],
        [keep, received, far],
        rows * shards * groups,
        share,
    )
    return result.reshape(-1, 1, share)


def solution(mesh):
    placed = (P(("bank", "gal"), None), P("gal", None), P(("bank", "gal"), None))
    return jax.shard_map(
        local, mesh=mesh, in_specs=placed, out_specs=P(None, "gal", "bank"), check_vma=False
    )
```

time: 133 us -> 45.9 us (0.35)
  blocking collectives: 83.6 us -> 0 us
  Pallas kernels: 0 us -> 19.6 us
  starting transfers between devices: 0.01 us -> 15.3 us
  other arithmetic: 14.2 us -> 0.01 us
  between operations: 13.5 us -> 0.08 us
  matrix products: 11.5 us -> 0 us
  waiting for transfers between devices: 0.02 us -> 6.8 us
  local copies, waits for them, and re-layouts: 9.9 us -> 3.81 us
    all_gather x1 -> x0, blocking collectives: 73.3 us -> none  [local(): every_test = lax.all_gather(tests, ('bank', 'gal'), axis=0, tiled=True)]
    pallas_call x0 -> x6, Pallas kernels: none -> 19.6 us  [the longest x2 9.33 us: more_sums(): pl.pallas_call(kernel, grid=(clips // block,), in_specs=[pl.BlockSpec((bl...]
    ppermute x0 -> x12, starting transfers between devices: none -> 15.3 us  [swap(): return lax.ppermute(values, axis, [(i, i ^ mask) for i in range(size)])]
    dot_general x3 -> x0, matrix products: 11.5 us -> none  [the longest x2 9.53 us: one_block(): sims = jnp.dot(block, clips_t, preferred_element_type=jnp.float32)]
    psum x1 -> x0, blocking collectives: 10.3 us -> none  [local(): totals = lax.psum(partial_sums, 'bank')]
    ppermute x0 -> x12, waiting for transfers between devices: none -> 6.8 us  [swap(): return lax.ppermute(values, axis, [(i, i ^ mask) for i in range(size)])]
    transpose x1 -> x0, other arithmetic: 5.4 us -> none  [local(): clips_t = unit_rows(gallery).T]
    convert_element_type x3 -> x0, other arithmetic: 4.54 us -> none  [unit_rows(): (wide * lax.rsqrt(jnp.sum(wide * wide, axis=-1, keepdims=True) + epsilon)...]
  transfers between devices with their start and end apart: 1 -> 12, of which waited for: 0 -> 3; matrix products, arithmetic and copies ran while one was open for 13% -> 0% of each run, Pallas kernels for 0% -> 28%
where the time goes in v1:
time: 45.9 us; the launch traced here: 45.7 us
  Pallas kernels  19.6 us (43%)
  starting transfers between devices  15.3 us (33%)
  waiting for transfers between devices  6.8 us (15%)
  local copies, waits for them, and re-layouts  3.81 us (8%)
    ppermute x12, starting transfers between devices, swap(): return lax.ppermute(values, axis, [(i, i ^ mask) for i in range(size)])  15.3 us
    pallas_call x2, Pallas kernels, more_sums(): pl.pallas_call(kernel, grid=(clips // block,), in_specs=[pl.BlockSpec((bl...  9.33 us
    ppermute x12, waiting for transfers between devices, swap(): return lax.ppermute(values, axis, [(i, i ^ mask) for i in range(size)])  6.8 us
    unnamed x6, local copies, waits for them, and re-layouts  3.81 us
    pallas_call x1, Pallas kernels, first_sums(): pl.pallas_call(kernel, grid_spec=pltpu.PrefetchScalarGridSpec(num_scalar_...  3.56 us
    pallas_call x1, Pallas kernels, last_sums(): pl.pallas_call(kernel, grid_spec=pltpu.PrefetchScalarGridSpec(num_scalar_...  3.46 us
    pallas_call x1, Pallas kernels, scores(): pl.pallas_call(kernel, grid_spec=pltpu.PrefetchScalarGridSpec(num_scalar_...  3.18 us
  transfers between devices with their start and end apart: 12, of which 3 were waited for; matrix products, arithmetic and copies ran while one was open for 0% of the time, Pallas kernels for 28%

profile of v1, /device:TPU:0, one launch (start us, length us, event | category | flops | bytes accessed | tf_op | source)
XLA Modules:
  0.0 45.7 jit_solution(3284202499522204759)
XLA Ops:
  0.0 0.9 %copy-done.1 = bf16[128,512]{1,0:T(8,128)(2,1)S(1)} copy-done((bf16[128,512]{1,0:T(8,128)(2,1)S(1)}, bf16[128,512]{1,0:T(8,128)(2,1)}, u32[]{:S(2)}) %copy-start.1) | copy-done | bytes 131096
  0.9 0.7 %copy-done.2 = bf16[16,512]{1,0:T(8,128)(2,1)S(1)} copy-done((bf16[16,512]{1,0:T(8,128)(2,1)S(1)}, bf16[16,512]{1,0:T(8,128)(2,1)}, u32[]{:S(2)}) %copy-start.2) | copy-done | bytes 16408
  1.6 0.1 prepare.1.payload_ref.refs_3_
  1.7 5.1 %collective-permute-start.2 = (bf16[144,512]{1,0:T(8,128)(2,1)S(1)}, bf16[144,512]{1,0:T(8,128)(2,1)S(1)}, u32[]{:S(2)}, u32[]{:S(2)}) collective-permute-start(bf16[144,512]{1,0:T(8,128)(2,1)S(1)} %prepare.1.payload_ref.refs_3_), channel_id=1, source_target_pairs={{0,6},{1,7},{2,4},{3,5},{4,2},{5,3},{6,0},{7,1},{8,14},{9,15},{10,... | collective-permute-start | bytes 442376 | tf_op jit(solution)/shard_map/ppermute | solution.py:215
  6.9 0.0 collective-permute-start
  6.9 1.7 %collective-permute-start.6 = (bf16[144,512]{1,0:T(8,128)(2,1)S(1)}, bf16[144,512]{1,0:T(8,128)(2,1)S(1)}, u32[]{:S(2)}, u32[]{:S(2)}) collective-permute-start(bf16[144,512]{1,0:T(8,128)(2,1)S(1)} %prepare.1.payload_ref.refs_3_), channel_id=1, source_target_pairs={{0,3},{1,2},{2,1},{3,0},{4,7},{5,6},{6,5},{7,4},{8,11},{9,10},{10,... | collective-permute-start | bytes 442376 | tf_op jit(solution)/shard_map/ppermute | solution.py:215
  8.6 1.2 %collective-permute-start.5 = (bf16[144,512]{1,0:T(8,128)(2,1)S(1)}, bf16[144,512]{1,0:T(8,128)(2,1)S(1)}, u32[]{:S(2)}, u32[]{:S(2)}) collective-permute-start(bf16[144,512]{1,0:T(8,128)(2,1)S(1)} %prepare.1.payload_ref.refs_3_), channel_id=1, source_target_pairs={{0,2},{1,3},{2,0},{3,1},{4,6},{5,7},{6,4},{7,5},{8,10},{9,11},{10,... | collective-permute-start | bytes 442376 | tf_op jit(solution)/shard_map/ppermute | solution.py:215
  9.8 0.5 %collective-permute-start.4 = (bf16[144,512]{1,0:T(8,128)(2,1)S(1)}, bf16[144,512]{1,0:T(8,128)(2,1)S(1)}, u32[]{:S(2)}, u32[]{:S(2)}) collective-permute-start(bf16[144,512]{1,0:T(8,128)(2,1)S(1)} %prepare.1.payload_ref.refs_3_), channel_id=1, source_target_pairs={{0,1},{1,0},{2,3},{3,2},{4,5},{5,4},{6,7},{7,6},{8,9},{9,8},{10,11... | collective-permute-start | bytes 442376 | tf_op jit(solution)/shard_map/ppermute | solution.py:215
  10.4 2.2 %copy-done = bf16[4096,512]{1,0:T(8,128)(2,1)S(1)} copy-done((bf16[4096,512]{1,0:T(8,128)(2,1)S(1)}, bf16[4096,512]{1,0:T(8,128)(2,1)}, u32[]{:S(2)}) %copy-start) | copy-done | bytes 4194328
  12.5 3.6 %first_sums.1 = (bf16[4096,512]{1,0:T(8,128)(2,1)S(1)}, f32[8,4096]{1,0:T(8,128)S(1)}) custom-call(s32[1]{0:T(128)} %bitcast.bank_ref, bf16[4096,512]{1,0:T(8,128)(2,1)S(1)} %copy-done, bf16[144,512]{1,0:T(8,128)(2,1)S(1)} %prepare.1.payload_ref.refs_3_), custom_call_target="tpu_custom_call" | custom-call | flops 536870912 | bytes 8388608 | tf_op jit(solution)/shard_map/first_sums/pallas_call | solution.py:59
  16.1 0.0 collective-permute-done.2.refs_1_.refs_9_
  16.1 1.6 %collective-permute-start.3 = (bf16[144,512]{1,0:T(8,128)(2,1)S(1)}, bf16[144,512]{1,0:T(8,128)(2,1)S(1)}, u32[]{:S(2)}, u32[]{:S(2)}) collective-permute-start(bf16[144,512]{1,0:T(8,128)(2,1)S(1)} %collective-permute-done.2.refs_1_.refs_9_), channel_id=1, source_target_pairs={{0,1},{1,0},{2,3},{3,2},{4,5},{5,4},{6,7},{7,6},{8,9},{9,8},{10,11... | collective-permute-start | bytes 442376 | tf_op jit(solution)/shard_map/ppermute | solution.py:215
  17.7 1.8 %collective-permute-done.refs_0_.refs_7_ = bf16[144,512]{1,0:T(8,128)(2,1)S(1)} collective-permute-done((bf16[144,512]{1,0:T(8,128)(2,1)S(1)}, bf16[144,512]{1,0:T(8,128)(2,1)S(1)}, u32[]{:S(2)}, u32[]{:S(2)}) %collective-permute-start) | collective-permute-done | bytes 147488 | tf_op jit(solution)/shard_map/ppermute | solution.py:215
  19.4 1.5 %collective-permute-start.1 = (bf16[144,512]{1,0:T(8,128)(2,1)S(1)}, bf16[144,512]{1,0:T(8,128)(2,1)S(1)}, u32[]{:S(2)}, u32[]{:S(2)}) collective-permute-start(bf16[144,512]{1,0:T(8,128)(2,1)S(1)} %collective-permute-done.refs_0_.refs_7_), channel_id=1, source_target_pairs={{0,1},{1,0},{2,3},{3,2},{4,5},{5,4},{6,7},{7,6},{8,9},{9,8},{10,11... | collective-permute-start | bytes 442376 | tf_op jit(solution)/shard_map/ppermute | solution.py:215
  20.9 0.0 collective-permute-done.6.refs_2_.refs_6_
  20.9 0.0 collective-permute-done.5.refs_1_.refs_5_
  20.9 0.0 collective-permute-done.4.refs_0_.refs_4_
  20.9 5.3 %more_sums.2.refs_2_ = f32[8,4096]{1,0:T(8,128)S(1)} custom-call(bf16[4096,512]{1,0:T(8,128)(2,1)S(1)} %get-tuple-element.10.unit_ref, bf16[144,512]{1,0:T(8,128)(2,1)S(1)} %collective-permute-done.4.refs_0_.refs_4_, bf16[144,512]{1,0:T(8,128)(2,1)S(1)} %collective-permute-done.5.refs_1_.refs_5_, ...), custom_call_target="tpu_custom_call" | custom-call | flops 1610612736 | bytes 4194304 | tf_op jit(solution)/shard_map/more_sums/pallas_call | solution.py:96
  26.3 4.0 %more_sums.3.refs_2_ = f32[8,4096]{1,0:T(8,128)S(1)} custom-call(bf16[4096,512]{1,0:T(8,128)(2,1)S(1)} %get-tuple-element.10.unit_ref, bf16[144,512]{1,0:T(8,128)(2,1)S(1)} %collective-permute-done.refs_0_.refs_7_, bf16[144,512]{1,0:T(8,128)(2,1)S(1)} %collective-permute-done.2.refs_1_.refs_9_, f32[8,4096]{1,0:T(8,128)S(1)} %more_sums.2.refs_2_), custom_call_target="tpu_custom_call" | custom-call | flops 1073741824 | bytes 4194304 | tf_op jit(solution)/shard_map/more_sums/pallas_call | solution.py:96
  30.3 0.0 collective-permute-done.3.refs_1_.refs_10_
  30.3 0.0 collective-permute-done.1.refs_0_.refs_8_
  30.3 3.5 %last_sums.1 = (f32[2,1024]{1,0:T(2,128)S(1)}, f32[2,1024]{1,0:T(2,128)S(1)}, bf16[128,512]{1,0:T(8,128)(2,1)S(1)}) custom-call(s32[1]{0:T(128)} %bitcast.1.gal_ref, bf16[4096,512]{1,0:T(8,128)(2,1)S(1)} %get-tuple-element.10.unit_ref, bf16[144,512]{1,0:T(8,128)(2,1)S(1)} %collective-permute-done.1.refs_0_.refs_8_, ...), custom_call_target="tpu_custom_call" | custom-call | flops 1073741824 | bytes 4194304 | tf_op jit(solution)/shard_map/last_sums/pallas_call | solution.py:140
  33.8 1.6 %collective-permute-start.8 = (bf16[128,512]{1,0:T(8,128)(2,1)S(1)}, bf16[128,512]{1,0:T(8,128)(2,1)S(1)}, u32[]{:S(2)}, u32[]{:S(2)}) collective-permute-start(bf16[128,512]{1,0:T(8,128)(2,1)S(1)} %get-tuple-element.12.refs_0_), channel_id=1, source_target_pairs={{0,16},{8,24},{16,0},{24,8},{1,17},{9,25},{17,1},{25,9},{2,18},{10... | collective-permute-start | bytes 393224 | tf_op jit(solution)/shard_map/ppermute | solution.py:215
  35.4 0.5 %collective-permute-start.7 = (bf16[128,512]{1,0:T(8,128)(2,1)S(1)}, bf16[128,512]{1,0:T(8,128)(2,1)S(1)}, u32[]{:S(2)}, u32[]{:S(2)}) collective-permute-start(bf16[128,512]{1,0:T(8,128)(2,1)S(1)} %get-tuple-element.12.refs_0_), channel_id=1, source_target_pairs={{0,8},{8,0},{16,24},{24,16},{1,9},{9,1},{17,25},{25,17},{2,10},{10... | collective-permute-start | bytes 393224 | tf_op jit(solution)/shard_map/ppermute | solution.py:215
  35.9 2.9 %collective-permute-done.8.refs_2_ = bf16[128,512]{1,0:T(8,128)(2,1)S(1)} collective-permute-done((bf16[128,512]{1,0:T(8,128)(2,1)S(1)}, bf16[128,512]{1,0:T(8,128)(2,1)S(1)}, u32[]{:S(2)}, u32[]{:S(2)}) %collective-permute-start.8) | collective-permute-done | bytes 131104 | tf_op jit(solution)/shard_map/ppermute | solution.py:215
  38.8 0.0 collective-permute-start.9
  38.8 0.0 collective-permute-done.10.refs_5_
  38.8 1.6 %collective-permute-start.11 = (f32[1,1024]{1,0:T(1,128)S(1)}, f32[1,1024]{1,0:T(1,128)S(1)}, u32[]{:S(2)}, u32[]{:S(2)}) collective-permute-start(f32[1,1024]{1,0:T(1,128)S(1)} %slice_add_fusion), channel_id=1, source_target_pairs={{0,16},{8,24},{16,0},{24,8},{1,17},{9,25},{17,1},{25,9},{2,18},{10... | collective-permute-start | bytes 12296 | tf_op jit(solution)/shard_map/ppermute | solution.py:215
  40.4 2.1 %collective-permute-done.11.refs_6_ = f32[1,1024]{1,0:T(1,128)S(1)} collective-permute-done((f32[1,1024]{1,0:T(1,128)S(1)}, f32[1,1024]{1,0:T(1,128)S(1)}, u32[]{:S(2)}, u32[]{:S(2)}) %collective-permute-start.11) | collective-permute-done | bytes 4128 | tf_op jit(solution)/shard_map/ppermute | solution.py:215
  42.5 0.0 collective-permute-done.7.refs_1_
  42.5 0.0 collective-permute-done.9.refs_3_
  42.5 3.2 %scores.1 = f32[4096,128]{1,0:T(8,128)} custom-call(s32[1]{0:T(128)} %bitcast.bank_ref, bf16[4096,512]{1,0:T(8,128)(2,1)S(1)} %get-tuple-element.10.unit_ref, bf16[128,512]{1,0:T(8,128)(2,1)S(1)} %get-tuple-element.12.refs_0_, bf16[128,512]{1,0:T(8,128)(2,1)S(1)} %collective-permute-done.7.refs_1_, bf16[128,512]{1,0:T(8,128)(2,1)S(1)} %collective-permute-done.8.refs_2_, ...), custom_call_target="tpu_custom_call" | custom-call | flops 536870912 | bytes 2097152 | tf_op jit(solution)/shard_map/scores/pallas_call | solution.py:194
  (5 shorter events, 0.0 us)
Async XLA Ops:
  0.0 0.9 %copy-start.1 = (bf16[128,512]{1,0:T(8,128)(2,1)S(1)}, bf16[128,512]{1,0:T(8,128)(2,1)}, u32[]{:S(2)}) copy-start(bf16[128,512]{1,0:T(8,128)(2,1)} %captions_ref.1) | copy-start | bytes 393220
  0.9 0.7 %copy-start.2 = (bf16[16,512]{1,0:T(8,128)(2,1)S(1)}, bf16[16,512]{1,0:T(8,128)(2,1)}, u32[]{:S(2)}) copy-start(bf16[16,512]{1,0:T(8,128)(2,1)} %tests_ref.1) | copy-start | bytes 49156
  1.7 14.4 %collective-permute-start.2 = (bf16[144,512]{1,0:T(8,128)(2,1)S(1)}, bf16[144,512]{1,0:T(8,128)(2,1)S(1)}, u32[]{:S(2)}, u32[]{:S(2)}) collective-permute-start(bf16[144,512]{1,0:T(8,128)(2,1)S(1)} %prepare.1.payload_ref.refs_3_), channel_id=1, source_target_pairs={{0,6},{1,7},{2,4},{3,5},{4,2},{5,3},{6,0},{7,1},{8,14},{9,15},{10,... | collective-permute-start | bytes 442376 | tf_op jit(solution)/shard_map/ppermute | solution.py:215
  6.9 12.6 %collective-permute-start = (bf16[144,512]{1,0:T(8,128)(2,1)S(1)}, bf16[144,512]{1,0:T(8,128)(2,1)S(1)}, u32[]{:S(2)}, u32[]{:S(2)}) collective-permute-start(bf16[144,512]{1,0:T(8,128)(2,1)S(1)} %prepare.1.payload_ref.refs_3_), channel_id=1, source_target_pairs={{0,4},{1,5},{2,6},{3,7},{4,0},{5,1},{6,2},{7,3},{8,12},{9,13},{10,... | collective-permute-start | bytes 442376 | tf_op jit(solution)/shard_map/ppermute | solution.py:215
  6.9 14.1 %collective-permute-start.6 = (bf16[144,512]{1,0:T(8,128)(2,1)S(1)}, bf16[144,512]{1,0:T(8,128)(2,1)S(1)}, u32[]{:S(2)}, u32[]{:S(2)}) collective-permute-start(bf16[144,512]{1,0:T(8,128)(2,1)S(1)} %prepare.1.payload_ref.refs_3_), channel_id=1, source_target_pairs={{0,3},{1,2},{2,1},{3,0},{4,7},{5,6},{6,5},{7,4},{8,11},{9,10},{10,... | collective-permute-start | bytes 442376 | tf_op jit(solution)/shard_map/ppermute | solution.py:215
  8.6 12.4 %collective-permute-start.5 = (bf16[144,512]{1,0:T(8,128)(2,1)S(1)}, bf16[144,512]{1,0:T(8,128)(2,1)S(1)}, u32[]{:S(2)}, u32[]{:S(2)}) collective-permute-start(bf16[144,512]{1,0:T(8,128)(2,1)S(1)} %prepare.1.payload_ref.refs_3_), channel_id=1, source_target_pairs={{0,2},{1,3},{2,0},{3,1},{4,6},{5,7},{6,4},{7,5},{8,10},{9,11},{10,... | collective-permute-start | bytes 442376 | tf_op jit(solution)/shard_map/ppermute | solution.py:215
  9.8 11.1 %collective-permute-start.4 = (bf16[144,512]{1,0:T(8,128)(2,1)S(1)}, bf16[144,512]{1,0:T(8,128)(2,1)S(1)}, u32[]{:S(2)}, u32[]{:S(2)}) collective-permute-start(bf16[144,512]{1,0:T(8,128)(2,1)S(1)} %prepare.1.payload_ref.refs_3_), channel_id=1, source_target_pairs={{0,1},{1,0},{2,3},{3,2},{4,5},{5,4},{6,7},{7,6},{8,9},{9,8},{10,11... | collective-permute-start | bytes 442376 | tf_op jit(solution)/shard_map/ppermute | solution.py:215
  10.3 2.2 %copy-start = (bf16[4096,512]{1,0:T(8,128)(2,1)S(1)}, bf16[4096,512]{1,0:T(8,128)(2,1)}, u32[]{:S(2)}) copy-start(bf16[4096,512]{1,0:T(8,128)(2,1)} %gallery_ref.1) | copy-start | bytes 12582916
  16.1 14.2 %collective-permute-start.3 = (bf16[144,512]{1,0:T(8,128)(2,1)S(1)}, bf16[144,512]{1,0:T(8,128)(2,1)S(1)}, u32[]{:S(2)}, u32[]{:S(2)}) collective-permute-start(bf16[144,512]{1,0:T(8,128)(2,1)S(1)} %collective-permute-done.2.refs_1_.refs_9_), channel_id=1, source_target_pairs={{0,1},{1,0},{2,3},{3,2},{4,5},{5,4},{6,7},{7,6},{8,9},{9,8},{10,11... | collective-permute-start | bytes 442376 | tf_op jit(solution)/shard_map/ppermute | solution.py:215
  19.4 10.9 %collective-permute-start.1 = (bf16[144,512]{1,0:T(8,128)(2,1)S(1)}, bf16[144,512]{1,0:T(8,128)(2,1)S(1)}, u32[]{:S(2)}, u32[]{:S(2)}) collective-permute-start(bf16[144,512]{1,0:T(8,128)(2,1)S(1)} %collective-permute-done.refs_0_.refs_7_), channel_id=1, source_target_pairs={{0,1},{1,0},{2,3},{3,2},{4,5},{5,4},{6,7},{7,6},{8,9},{9,8},{10,11... | collective-permute-start | bytes 442376 | tf_op jit(solution)/shard_map/ppermute | solution.py:215
  33.8 5.0 %collective-permute-start.8 = (bf16[128,512]{1,0:T(8,128)(2,1)S(1)}, bf16[128,512]{1,0:T(8,128)(2,1)S(1)}, u32[]{:S(2)}, u32[]{:S(2)}) collective-permute-start(bf16[128,512]{1,0:T(8,128)(2,1)S(1)} %get-tuple-element.12.refs_0_), channel_id=1, source_target_pairs={{0,16},{8,24},{16,0},{24,8},{1,17},{9,25},{17,1},{25,9},{2,18},{10... | collective-permute-start | bytes 393224 | tf_op jit(solution)/shard_map/ppermute | solution.py:215
  35.4 3.4 %collective-permute-start.10 = (f32[2,1024]{1,0:T(2,128)S(1)}, f32[2,1024]{1,0:T(2,128)S(1)}, u32[]{:S(2)}, u32[]{:S(2)}) collective-permute-start(f32[2,1024]{1,0:T(2,128)S(1)} %get-tuple-element.14), channel_id=1, source_target_pairs={{0,8},{8,0},{16,24},{24,16},{1,9},{9,1},{17,25},{25,17},{2,10},{10... | collective-permute-start | bytes 24584 | tf_op jit(solution)/shard_map/ppermute | solution.py:215
  35.4 7.1 %collective-permute-start.7 = (bf16[128,512]{1,0:T(8,128)(2,1)S(1)}, bf16[128,512]{1,0:T(8,128)(2,1)S(1)}, u32[]{:S(2)}, u32[]{:S(2)}) collective-permute-start(bf16[128,512]{1,0:T(8,128)(2,1)S(1)} %get-tuple-element.12.refs_0_), channel_id=1, source_target_pairs={{0,8},{8,0},{16,24},{24,16},{1,9},{9,1},{17,25},{25,17},{2,10},{10... | collective-permute-start | bytes 393224 | tf_op jit(solution)/shard_map/ppermute | solution.py:215
  38.8 3.7 %collective-permute-start.9 = (bf16[128,512]{1,0:T(8,128)(2,1)S(1)}, bf16[128,512]{1,0:T(8,128)(2,1)S(1)}, u32[]{:S(2)}, u32[]{:S(2)}) collective-permute-start(bf16[128,512]{1,0:T(8,128)(2,1)S(1)} %collective-permute-done.8.refs_2_), channel_id=1, source_target_pairs={{0,8},{8,0},{16,24},{24,16},{1,9},{9,1},{17,25},{25,17},{2,10},{10... | collective-permute-start | bytes 393224 | tf_op jit(solution)/shard_map/ppermute | solution.py:215
  38.8 3.7 %collective-permute-start.11 = (f32[1,1024]{1,0:T(1,128)S(1)}, f32[1,1024]{1,0:T(1,128)S(1)}, u32[]{:S(2)}, u32[]{:S(2)}) collective-permute-start(f32[1,1024]{1,0:T(1,128)S(1)} %slice_add_fusion), channel_id=1, source_target_pairs={{0,16},{8,24},{16,0},{24,8},{1,17},{9,25},{17,1},{25,9},{2,18},{10... | collective-permute-start | bytes 12296 | tf_op jit(solution)/shard_map/ppermute | solution.py:215

commit v2 on v0

v2 whole, which is shorter than its diff:
```python
import jax
import jax.numpy as jnp
from jax import lax
from jax.experimental import pallas as pl
from jax.experimental.pallas import tpu as pltpu
from jax.sharding import PartitionSpec as P

inverse_temp = 20.0
epsilon = 1e-06
log2_e = 1.4426950408889634
lanes = 128
in_vmem = pl.BlockSpec(memory_space=pltpu.VMEM)
in_smem = pl.BlockSpec(memory_space=pltpu.SMEM)
in_hbm = pl.BlockSpec(memory_space=pltpu.HBM)


def unit_rows(values):
    wide = values.astype(jnp.float32)
    return (wide * lax.rsqrt(jnp.sum(wide * wide, axis=-1, keepdims=True) + epsilon)).astype(
        jnp.bfloat16
    )


def products(left, right):
    return lax.dot_general(
        left, right, (((1,), (1,)), ((), ())), preferred_element_type=jnp.float32
    )


def exp_sums(captions, clips):
    grown = jnp.exp2(products(captions, clips) * (inverse_temp * log2_e))
    return jnp.sum(grown.reshape(grown.shape[0] // 8, 8, grown.shape[1]), axis=0)


def call(kernel, name, out_shape, flops, moved, *args, in_specs, out_specs=in_vmem, scratch=()):
    return pl.pallas_call(
        kernel,
        out_shape=out_shape,
        in_specs=in_specs,
        out_specs=out_specs,
        scratch_shapes=list(scratch),
        cost_estimate=pl.CostEstimate(flops=flops, bytes_accessed=moved, transcendentals=0),
        compiler_params=pltpu.CompilerParams(vmem_limit_bytes=32 * 1024 * 1024),
        name=name,
    )(*args)


def stay_in_hbm(values):
    return pltpu.with_memory_space_constraint(values, pltpu.HBM)


def prepare(captions, tests):
    rows, more, width = captions.shape[0], tests.shape[0], captions.shape[1]

    def kernel(captions_ref, tests_ref, out_ref, captions_in, tests_in, sems):
        first = pltpu.make_async_copy(captions_ref, captions_in, sems.at[0])
        second = pltpu.make_async_copy(tests_ref, tests_in, sems.at[1])
        first.start()
        second.start()
        second.wait()
        out_ref[rows:, :] = unit_rows(tests_in[...])
        first.wait()
        out_ref[:rows, :] = unit_rows(captions_in[...])

    return call(
        kernel,
        "prepare",
        jax.ShapeDtypeStruct((rows + more, width), jnp.bfloat16),
        rows * width,
        rows * width * 4,
        stay_in_hbm(captions),
        stay_in_hbm(tests),
        in_specs=[in_hbm] * 2,
        scratch=[
            pltpu.VMEM(captions.shape, captions.dtype),
            pltpu.VMEM(tests.shape, tests.dtype),
            pltpu.SemaphoreType.DMA((2,)),
        ],
    )


def unit_gallery(bank, gallery, share):
    clips, width = gallery.shape
    quarters = clips // share

    def kernel(bank_ref, gallery_ref, out_ref, arrived, sems):
        half = share // 2
        copies = []
        for k in range(2 * quarters):
            begin = pl.multiple_of(((k // 2) ^ bank_ref[0]) * share + k % 2 * half, half)
            copies.append(
                pltpu.make_async_copy(gallery_ref.at[pl.ds(begin, half)], arrived.at[k], sems.at[k])
            )
            copies[k].start()
        for k in range(2 * quarters):
            copies[k].wait()
            out_ref[k * half : (k + 1) * half, :] = unit_rows(arrived[k])

    return call(
        kernel,
        "unit_gallery",
        jax.ShapeDtypeStruct((clips, width), jnp.bfloat16),
        4 * clips * width,
        4 * clips * width,
        bank,
        stay_in_hbm(gallery),
        in_specs=[in_smem, in_hbm],
        scratch=[
            pltpu.VMEM((2 * quarters, share // 2, width), gallery.dtype),
            pltpu.SemaphoreType.DMA((2 * quarters,)),
        ],
    )


def first_sums(unit, payloads, rows):
    clips, width = unit.shape
    count = len(payloads)

    def kernel(unit_ref, *refs):
        captions = jnp.concatenate([ref[:rows, :] for ref in refs[:count]], axis=0)
        refs[count][...] = exp_sums(captions, unit_ref[...])

    return call(
        kernel,
        "first_sums",
        jax.ShapeDtypeStruct((8, clips), jnp.float32),
        2 * rows * clips * width * count,
        2 * clips * width,
        unit,
        *payloads,
        in_specs=[in_vmem] * (count + 1),
    )


def last_sums(unit, payloads, sums, rows, share):
    clips, width = unit.shape
    count, parts = len(payloads), len(sums)
    half = clips // share // 2

    def kernel(unit_ref, *refs):
        captions = jnp.concatenate([ref[:rows, :] for ref in refs[:count]], axis=0)
        total = exp_sums(captions, unit_ref[...])
        for ref in refs[count : count + parts]:
            total = total + ref[...]
        total = jnp.sum(total, axis=0, keepdims=True)
        keep_ref, send_ref = refs[count + parts :]
        for k in range(half):
            keep_ref[k : k + 1, :] = total[:, 2 * k * share : (2 * k + 1) * share]
            send_ref[k : k + 1, :] = total[:, (2 * k + 1) * share : (2 * k + 2) * share]

    return call(
        kernel,
        "last_sums",
        [jax.ShapeDtypeStruct((half, share), jnp.float32)] * 2,
        2 * rows * clips * width * count,
        2 * clips * width,
        unit,
        *payloads,
        *sums,
        in_specs=[in_vmem] * (1 + count + parts),
        out_specs=[in_vmem] * 2,
    )


def gather_tests(gal, payloads, rows):
    total, width = payloads[0].shape
    more, count = total - rows, len(payloads)

    def kernel(gal_ref, *refs):
        for mask in range(count):
            place = pl.multiple_of((gal_ref[0] ^ mask) * more, more)
            refs[count][pl.ds(place, more), :] = refs[mask][rows:, :]

    return call(
        kernel,
        "gather_tests",
        jax.ShapeDtypeStruct((count * more, width), jnp.bfloat16),
        0,
        4 * count * more * width,
        gal,
        *payloads,
        in_specs=[in_smem] + [in_vmem] * count,
    )


def raw_scores(unit, tests, share):
    rows, width = tests[0].shape
    count = len(tests)

    def kernel(unit_ref, *refs):
        every = jnp.concatenate([ref[...] for ref in refs[:count]], axis=0)
        refs[count][...] = inverse_temp * products(every, unit_ref[:share, :])

    return call(
        kernel,
        "raw_scores",
        jax.ShapeDtypeStruct((count * rows, share), jnp.float32),
        2 * count * rows * share * width,
        4 * count * rows * share,
        unit,
        *tests,
        in_specs=[in_vmem] * (1 + count),
    )


def write_scores(bank, raw, keep, received, far, groups, total):
    every, share = raw.shape
    rows, per_row = every // groups, share // lanes

    def kernel(bank_ref, raw_ref, keep_ref, received_ref, far_ref, out_ref, staged, sems):
        normalizer = keep_ref[0:1, :] + received_ref[0:1, :] + far_ref[...]
        shift = jnp.log(normalizer / total)
        copies = []
        for mask in range(groups):
            values = raw_ref[mask * rows : (mask + 1) * rows, :] - shift
            for k in range(per_row):
                staged[mask, pl.ds(k, rows, stride=per_row), :] = values[:, k * lanes : (k + 1) * lanes]
            begin = pl.multiple_of((bank_ref[0] ^ mask) * (rows * per_row), rows * per_row)
            copies.append(
                pltpu.make_async_copy(
                    staged.at[mask], out_ref.at[pl.ds(begin, rows * per_row)], sems.at[mask]
                )
            )
            copies[mask].start()
        for copy in copies:
            copy.wait()

    return call(
        kernel,
        "write_scores",
        jax.ShapeDtypeStruct((every * per_row, lanes), jnp.float32),
        every * share,
        8 * every * share,
        bank,
        raw,
        keep,
        received,
        far,
        in_specs=[in_smem] + [in_vmem] * 4,
        out_specs=in_hbm,
        scratch=[
            pltpu.VMEM((groups, rows * per_row, lanes), jnp.float32),
            pltpu.SemaphoreType.DMA((groups,)),
        ],
    )


def swap(values, axis, mask):
    size = lax.axis_size(axis)
    return lax.ppermute(values, axis, [(i, i ^ mask) for i in range(size)])


def after(values, other):
    return lax.optimization_barrier((values, other))[0]


def local(querybank, gallery, test_queries):
    groups, shards = lax.axis_size("bank"), lax.axis_size("gal")
    rows = querybank.shape[0]
    share = gallery.shape[0] // groups
    bank = lax.axis_index("bank").astype(jnp.int32)[None]
    gal = lax.axis_index("gal").astype(jnp.int32)[None]

    payload = prepare(querybank, test_queries)
    low = shards // 4
    got = {0: payload}
    for high in (2, 3, 1):
        got[high * low] = swap(payload, "gal", high * low)
    for mask in range(1, low):
        got[low + mask] = swap(payload, "gal", low + mask)
        got[mask] = swap(payload, "gal", mask)

    unit = unit_gallery(bank, gallery, share)
    sums = [first_sums(unit, [got[m] for m in range(2 * low)], rows)]
    for high in (2, 3):
        here = after(got[high * low], sums[0])
        for mask in range(1, low):
            got[high * low + mask] = swap(here, "gal", mask)
    sums.append(first_sums(unit, [got[2 * low], got[3 * low]], rows))

    for high in (2, 3):
        for mask in range(1, low):
            got[high * low + mask] = after(got[high * low + mask], sums[1])
    tests = gather_tests(gal, [got[m] for m in range(shards)], rows)
    tests_y = swap(tests, "bank", 2)
    tests_core = swap(tests, "bank", 1)
    last = [got[h * low + m] for h in (2, 3) for m in range(1, low)]
    keep, send = last_sums(unit, last, sums, rows, share)
    received = swap(send, "bank", 1)
    far = swap(keep[1:] + received[1:], "bank", 2)
    tests_both = swap(after(tests_y, received), "bank", 1)
    raw = raw_scores(unit, [tests, tests_core, tests_y, tests_both], share)
    result = write_scores(bank, raw, keep, received, far, groups, rows * shards * groups)
    return result.reshape(-1, 1, share)


def solution(mesh):
    placed = (P(("bank", "gal"), None), P("gal", None), P(("bank", "gal"), None))
    return jax.shard_map(
        local, mesh=mesh, in_specs=placed, out_specs=P(None, "gal", "bank"), check_vma=False
    )
```

time: 133 us -> 38.5 us (0.29)
  blocking collectives: 83.6 us -> 0 us
  starting transfers between devices: 0.01 us -> 14.6 us
  other arithmetic: 14.2 us -> 0.01 us
  between operations: 13.5 us -> 0.09 us
  matrix products: 11.5 us -> 0 us
  Pallas kernels: 0 us -> 10.8 us
  waiting for transfers between devices: 0.02 us -> 8.67 us
  local copies, waits for them, and re-layouts: 9.9 us -> 4.14 us
    all_gather x1 -> x0, blocking collectives: 73.3 us -> none  [local(): every_test = lax.all_gather(tests, ('bank', 'gal'), axis=0, tiled=True)]
    ppermute x0 -> x12, starting transfers between devices: none -> 14.6 us  [swap(): return lax.ppermute(values, axis, [(i, i ^ mask) for i in range(size)])]
    dot_general x3 -> x0, matrix products: 11.5 us -> none  [the longest x2 9.53 us: one_block(): sims = jnp.dot(block, clips_t, preferred_element_type=jnp.float32)]
    pallas_call x0 -> x8, Pallas kernels: none -> 10.8 us  [call(): pl.pallas_call(kernel, out_shape=out_shape, in_specs=in_specs, out_specs=...]
    psum x1 -> x0, blocking collectives: 10.3 us -> none  [local(): totals = lax.psum(partial_sums, 'bank')]
    ppermute x0 -> x12, waiting for transfers between devices: none -> 8.67 us  [swap(): return lax.ppermute(values, axis, [(i, i ^ mask) for i in range(size)])]
    transpose x1 -> x0, other arithmetic: 5.4 us -> none  [local(): clips_t = unit_rows(gallery).T]
    convert_element_type x3 -> x0, other arithmetic: 4.54 us -> none  [unit_rows(): (wide * lax.rsqrt(jnp.sum(wide * wide, axis=-1, keepdims=True) + epsilon)...]
  transfers between devices with their start and end apart: 1 -> 12, of which waited for: 0 -> 7; matrix products, arithmetic and copies ran while one was open for 13% -> 0% of each run, Pallas kernels for 0% -> 22%
where the time goes in v2:
time: 38.5 us; the launch traced here: 38.3 us
  starting transfers between devices  14.6 us (38%)
  Pallas kernels  10.8 us (28%)
  waiting for transfers between devices  8.67 us (23%)
  local copies, waits for them, and re-layouts  4.14 us (11%)
    ppermute x12, starting transfers between devices, swap(): return lax.ppermute(values, axis, [(i, i ^ mask) for i in range(size)])  14.6 us
    pallas_call x8, Pallas kernels, call(): pl.pallas_call(kernel, out_shape=out_shape, in_specs=in_specs, out_specs=...  10.8 us
    ppermute x12, waiting for transfers between devices, swap(): return lax.ppermute(values, axis, [(i, i ^ mask) for i in range(size)])  8.67 us
    unnamed x6, local copies, waits for them, and re-layouts  4.14 us
  transfers between devices with their start and end apart: 12, of which 7 were waited for; matrix products, arithmetic and copies ran while one was open for 0% of the time, Pallas kernels for 22%

profile of v2, /device:TPU:0, one launch (start us, length us, event | category | flops | bytes accessed | tf_op | source)
XLA Modules:
  0.0 38.3 jit_solution(15638142548039643459)
XLA Ops:
  0.0 1.0 %prepare.1.refs_0_ = bf16[144,512]{1,0:T(8,128)(2,1)S(1)} custom-call(bf16[128,512]{1,0:T(8,128)(2,1)} %captions_ref.1, bf16[16,512]{1,0:T(8,128)(2,1)} %tests_ref.1), custom_call_target="tpu_custom_call" | custom-call | flops 65536 | bytes 262144 | tf_op jit(solution)/shard_map/prepare/pallas_call | solution.py:36
  1.0 3.0 %collective-permute-start = (bf16[144,512]{1,0:T(8,128)(2,1)S(1)}, bf16[144,512]{1,0:T(8,128)(2,1)S(1)}, u32[]{:S(2)}, u32[]{:S(2)}) collective-permute-start(bf16[144,512]{1,0:T(8,128)(2,1)S(1)} %prepare.1.refs_0_), channel_id=1, source_target_pairs={{0,1},{1,0},{2,3},{3,2},{4,5},{5,4},{6,7},{7,6},{8,9},{9,8},{10,11... | collective-permute-start | bytes 442376 | tf_op jit(solution)/shard_map/ppermute | solution.py:250
  4.0 1.6 %collective-permute-start.1 = (bf16[144,512]{1,0:T(8,128)(2,1)S(1)}, bf16[144,512]{1,0:T(8,128)(2,1)S(1)}, u32[]{:S(2)}, u32[]{:S(2)}) collective-permute-start(bf16[144,512]{1,0:T(8,128)(2,1)S(1)} %prepare.1.refs_0_), channel_id=1, source_target_pairs={{0,2},{1,3},{2,0},{3,1},{4,6},{5,7},{6,4},{7,5},{8,10},{9,11},{10,... | collective-permute-start | bytes 442376 | tf_op jit(solution)/shard_map/ppermute | solution.py:250
  5.6 0.0 collective-permute-start.2
  5.6 3.0 %collective-permute-start.3 = (bf16[144,512]{1,0:T(8,128)(2,1)S(1)}, bf16[144,512]{1,0:T(8,128)(2,1)S(1)}, u32[]{:S(2)}, u32[]{:S(2)}) collective-permute-start(bf16[144,512]{1,0:T(8,128)(2,1)S(1)} %prepare.1.refs_0_), channel_id=1, source_target_pairs={{0,4},{1,5},{2,6},{3,7},{4,0},{5,1},{6,2},{7,3},{8,12},{9,13},{10,... | collective-permute-start | bytes 442376 | tf_op jit(solution)/shard_map/ppermute | solution.py:250
  8.6 1.3 %collective-permute-start.5 = (bf16[144,512]{1,0:T(8,128)(2,1)S(1)}, bf16[144,512]{1,0:T(8,128)(2,1)S(1)}, u32[]{:S(2)}, u32[]{:S(2)}) collective-permute-start(bf16[144,512]{1,0:T(8,128)(2,1)S(1)} %prepare.1.refs_0_), channel_id=1, source_target_pairs={{0,6},{1,7},{2,4},{3,5},{4,2},{5,3},{6,0},{7,1},{8,14},{9,15},{10,... | collective-permute-start | bytes 442376 | tf_op jit(solution)/shard_map/ppermute | solution.py:250
  10.0 2.6 %unit_gallery.1.unit_ref = bf16[4096,512]{1,0:T(8,128)(2,1)S(1)} custom-call(s32[1]{0:T(128)} %bitcast.bank_ref, bf16[4096,512]{1,0:T(8,128)(2,1)} %gallery_ref.1), custom_call_target="tpu_custom_call" | custom-call | flops 8388608 | bytes 8388608 | tf_op jit(solution)/shard_map/unit_gallery/pallas_call | solution.py:36
  12.6 0.0 collective-permute-done.refs_1_
  12.6 1.4 %collective-permute-done.1.refs_2_ = bf16[144,512]{1,0:T(8,128)(2,1)S(1)} collective-permute-done((bf16[144,512]{1,0:T(8,128)(2,1)S(1)}, bf16[144,512]{1,0:T(8,128)(2,1)S(1)}, u32[]{:S(2)}, u32[]{:S(2)}) %collective-permute-start.1) | collective-permute-done | bytes 147488 | tf_op jit(solution)/shard_map/ppermute | solution.py:250
  14.0 1.5 %collective-permute-done.2.refs_3_ = bf16[144,512]{1,0:T(8,128)(2,1)S(1)} collective-permute-done((bf16[144,512]{1,0:T(8,128)(2,1)S(1)}, bf16[144,512]{1,0:T(8,128)(2,1)S(1)}, u32[]{:S(2)}, u32[]{:S(2)}) %collective-permute-start.2) | collective-permute-done | bytes 147488 | tf_op jit(solution)/shard_map/ppermute | solution.py:250
  15.5 2.4 %first_sums.2.refs_2_ = f32[8,4096]{1,0:T(8,128)S(1)} custom-call(bf16[4096,512]{1,0:T(8,128)(2,1)S(1)} %unit_gallery.1.unit_ref, bf16[144,512]{1,0:T(8,128)(2,1)S(1)} %prepare.1.refs_0_, bf16[144,512]{1,0:T(8,128)(2,1)S(1)} %collective-permute-done.refs_1_, bf16[144,512]{1,0:T(8,128)(2,1)S(1)} %collective-permute-done.1.refs_2_, ...), custom_call_target="tpu_custom_call" | custom-call | flops 2147483648 | bytes 4194304 | tf_op jit(solution)/shard_map/first_sums/pallas_call | solution.py:36
  17.9 1.9 %copy-done = bf16[4096,512]{1,0:T(8,128)(2,1)} copy-done((bf16[4096,512]{1,0:T(8,128)(2,1)}, bf16[4096,512]{1,0:T(8,128)(2,1)S(1)}, u32[]{:S(2)}) %copy-start) | copy-done | bytes 4194328
  19.8 0.0 collective-permute-done.3.refs_0_.refs_4_
  19.8 1.7 %collective-permute-start.4 = (bf16[144,512]{1,0:T(8,128)(2,1)S(1)}, bf16[144,512]{1,0:T(8,128)(2,1)S(1)}, u32[]{:S(2)}, u32[]{:S(2)}) collective-permute-start(bf16[144,512]{1,0:T(8,128)(2,1)S(1)} %collective-permute-done.3.refs_0_.refs_4_), channel_id=1, source_target_pairs={{0,1},{1,0},{2,3},{3,2},{4,5},{5,4},{6,7},{7,6},{8,9},{9,8},{10,11... | collective-permute-start | bytes 442376 | tf_op jit(solution)/shard_map/ppermute | solution.py:250
  21.5 0.0 collective-permute-done.5.refs_1_.refs_6_
  21.5 0.4 collective-permute-start.6
  21.8 2.2 %copy-done.1 = bf16[4096,512]{1,0:T(8,128)(2,1)S(1)} copy-done((bf16[4096,512]{1,0:T(8,128)(2,1)S(1)}, bf16[4096,512]{1,0:T(8,128)(2,1)}, u32[]{:S(2)}) %copy-start.1) | copy-done | bytes 4194328
  24.0 1.3 %first_sums.3.refs_3_ = f32[8,4096]{1,0:T(8,128)S(1)} custom-call(bf16[4096,512]{1,0:T(8,128)(2,1)S(1)} %copy-done.1, bf16[144,512]{1,0:T(8,128)(2,1)S(1)} %collective-permute-done.3.refs_0_.refs_4_, bf16[144,512]{1,0:T(8,128)(2,1)S(1)} %collective-permute-done.5.refs_1_.refs_6_), custom_call_target="tpu_custom_call" | custom-call | flops 1073741824 | bytes 4194304 | tf_op jit(solution)/shard_map/first_sums/pallas_call | solution.py:36
  25.3 1.1 %collective-permute-done.4.refs_5_.refs_0_ = bf16[144,512]{1,0:T(8,128)(2,1)S(1)} collective-permute-done((bf16[144,512]{1,0:T(8,128)(2,1)S(1)}, bf16[144,512]{1,0:T(8,128)(2,1)S(1)}, u32[]{:S(2)}, u32[]{:S(2)}) %collective-permute-start.4) | collective-permute-done | bytes 147488 | tf_op jit(solution)/shard_map/ppermute | solution.py:250
  26.5 1.6 %collective-permute-done.6.refs_7_.refs_1_ = bf16[144,512]{1,0:T(8,128)(2,1)S(1)} collective-permute-done((bf16[144,512]{1,0:T(8,128)(2,1)S(1)}, bf16[144,512]{1,0:T(8,128)(2,1)S(1)}, u32[]{:S(2)}, u32[]{:S(2)}) %collective-permute-start.6) | collective-permute-done | bytes 147488 | tf_op jit(solution)/shard_map/ppermute | solution.py:250
  28.1 1.5 %collective-permute-start.8 = (bf16[128,512]{1,0:T(8,128)(2,1)S(1)}, bf16[128,512]{1,0:T(8,128)(2,1)S(1)}, u32[]{:S(2)}, u32[]{:S(2)}) collective-permute-start(bf16[128,512]{1,0:T(8,128)(2,1)S(1)} %gather_tests.1.refs_0_), channel_id=1, source_target_pairs={{0,16},{8,24},{16,0},{24,8},{1,17},{9,25},{17,1},{25,9},{2,18},{10... | collective-permute-start | bytes 393224 | tf_op jit(solution)/shard_map/ppermute | solution.py:250
  29.6 1.3 %last_sums.1 = (f32[2,1024]{1,0:T(2,128)S(1)}, f32[2,1024]{1,0:T(2,128)S(1)}) custom-call(bf16[4096,512]{1,0:T(8,128)(2,1)S(1)} %copy-done.2, bf16[144,512]{1,0:T(8,128)(2,1)S(1)} %collective-permute-done.4.refs_5_.refs_0_, bf16[144,512]{1,0:T(8,128)(2,1)S(1)} %collective-permute-done.6.refs_7_.refs_1_, f32[8,4096]{1,0:T(8,128)S(1)} %first_sums.2.refs_2_, ...), custom_call_target="tpu_custom_call" | custom-call | flops 1073741824 | bytes 4194304 | tf_op jit(solution)/shard_map/last_sums/pallas_call | solution.py:36
  30.9 0.1 collective-permute-start.9
  31.0 0.5 %collective-permute-start.7 = (bf16[128,512]{1,0:T(8,128)(2,1)S(1)}, bf16[128,512]{1,0:T(8,128)(2,1)S(1)}, u32[]{:S(2)}, u32[]{:S(2)}) collective-permute-start(bf16[128,512]{1,0:T(8,128)(2,1)S(1)} %gather_tests.1.refs_0_), channel_id=1, source_target_pairs={{0,8},{8,0},{16,24},{24,16},{1,9},{9,1},{17,25},{25,17},{2,10},{10... | collective-permute-start | bytes 393224 | tf_op jit(solution)/shard_map/ppermute | solution.py:250
  31.5 0.7 %collective-permute-done.9.received_ref = f32[2,1024]{1,0:T(2,128)S(1)} collective-permute-done((f32[2,1024]{1,0:T(2,128)S(1)}, f32[2,1024]{1,0:T(2,128)S(1)}, u32[]{:S(2)}, u32[]{:S(2)}) %collective-permute-start.9) | collective-permute-done | bytes 8224 | tf_op jit(solution)/shard_map/ppermute | solution.py:250
  32.1 1.0 %collective-permute-done.8.refs_2_ = bf16[128,512]{1,0:T(8,128)(2,1)S(1)} collective-permute-done((bf16[128,512]{1,0:T(8,128)(2,1)S(1)}, bf16[128,512]{1,0:T(8,128)(2,1)S(1)}, u32[]{:S(2)}, u32[]{:S(2)}) %collective-permute-start.8) | collective-permute-done | bytes 131104 | tf_op jit(solution)/shard_map/ppermute | solution.py:250
  33.1 0.0 collective-permute-start.10
  33.1 1.5 %collective-permute-start.11 = (f32[1,1024]{1,0:T(1,128)S(1)}, f32[1,1024]{1,0:T(1,128)S(1)}, u32[]{:S(2)}, u32[]{:S(2)}) collective-permute-start(f32[1,1024]{1,0:T(1,128)S(1)} %slice_add_fusion), channel_id=1, source_target_pairs={{0,16},{8,24},{16,0},{24,8},{1,17},{9,25},{17,1},{25,9},{2,18},{10... | collective-permute-start | bytes 12296 | tf_op jit(solution)/shard_map/ppermute | solution.py:250
  34.6 0.0 collective-permute-done.7.refs_1_
  34.6 0.7 %raw_scores.1.raw_ref = f32[512,1024]{1,0:T(8,128)S(1)} custom-call(bf16[4096,512]{1,0:T(8,128)(2,1)S(1)} %copy-done.2, bf16[128,512]{1,0:T(8,128)(2,1)S(1)} %gather_tests.1.refs_0_, bf16[128,512]{1,0:T(8,128)(2,1)S(1)} %collective-permute-done.7.refs_1_, bf16[128,512]{1,0:T(8,128)(2,1)S(1)} %collective-permute-done.8.refs_2_, ...), custom_call_target="tpu_custom_call" | custom-call | flops 536870912 | bytes 2097152 | tf_op jit(solution)/shard_map/raw_scores/pallas_call | solution.py:36
  35.4 1.4 %collective-permute-done.11.far_ref = f32[1,1024]{1,0:T(1,128)S(1)} collective-permute-done((f32[1,1024]{1,0:T(1,128)S(1)}, f32[1,1024]{1,0:T(1,128)S(1)}, u32[]{:S(2)}, u32[]{:S(2)}) %collective-permute-start.11) | collective-permute-done | bytes 4128 | tf_op jit(solution)/shard_map/ppermute | solution.py:250
  36.8 1.5 %write_scores.1 = f32[4096,128]{1,0:T(8,128)} custom-call(s32[1]{0:T(128)} %bitcast.bank_ref, f32[512,1024]{1,0:T(8,128)S(1)} %raw_scores.1.raw_ref, f32[2,1024]{1,0:T(2,128)S(1)} %get-tuple-element.18.keep_ref, f32[2,1024]{1,0:T(2,128)S(1)} %collective-permute-done.9.received_ref, f32[1,1024]{1,0:T(1,128)S(1)} %collective-permute-done.11.far_ref), custom_call_target="tpu_custom_call" | custom-call | flops 524288 | bytes 4194304 | tf_op jit(solution)/shard_map/write_scores/pallas_call | solution.py:36
  (7 shorter events, 0.0 us)
Async XLA Ops:
  1.0 11.5 %collective-permute-start = (bf16[144,512]{1,0:T(8,128)(2,1)S(1)}, bf16[144,512]{1,0:T(8,128)(2,1)S(1)}, u32[]{:S(2)}, u32[]{:S(2)}) collective-permute-start(bf16[144,512]{1,0:T(8,128)(2,1)S(1)} %prepare.1.refs_0_), channel_id=1, source_target_pairs={{0,1},{1,0},{2,3},{3,2},{4,5},{5,4},{6,7},{7,6},{8,9},{9,8},{10,11... | collective-permute-start | bytes 442376 | tf_op jit(solution)/shard_map/ppermute | solution.py:250
  4.0 9.9 %collective-permute-start.1 = (bf16[144,512]{1,0:T(8,128)(2,1)S(1)}, bf16[144,512]{1,0:T(8,128)(2,1)S(1)}, u32[]{:S(2)}, u32[]{:S(2)}) collective-permute-start(bf16[144,512]{1,0:T(8,128)(2,1)S(1)} %prepare.1.refs_0_), channel_id=1, source_target_pairs={{0,2},{1,3},{2,0},{3,1},{4,6},{5,7},{6,4},{7,5},{8,10},{9,11},{10,... | collective-permute-start | bytes 442376 | tf_op jit(solution)/shard_map/ppermute | solution.py:250
  5.6 9.9 %collective-permute-start.2 = (bf16[144,512]{1,0:T(8,128)(2,1)S(1)}, bf16[144,512]{1,0:T(8,128)(2,1)S(1)}, u32[]{:S(2)}, u32[]{:S(2)}) collective-permute-start(bf16[144,512]{1,0:T(8,128)(2,1)S(1)} %prepare.1.refs_0_), channel_id=1, source_target_pairs={{0,3},{1,2},{2,1},{3,0},{4,7},{5,6},{6,5},{7,4},{8,11},{9,10},{10,... | collective-permute-start | bytes 442376 | tf_op jit(solution)/shard_map/ppermute | solution.py:250
  5.6 14.2 %collective-permute-start.3 = (bf16[144,512]{1,0:T(8,128)(2,1)S(1)}, bf16[144,512]{1,0:T(8,128)(2,1)S(1)}, u32[]{:S(2)}, u32[]{:S(2)}) collective-permute-start(bf16[144,512]{1,0:T(8,128)(2,1)S(1)} %prepare.1.refs_0_), channel_id=1, source_target_pairs={{0,4},{1,5},{2,6},{3,7},{4,0},{5,1},{6,2},{7,3},{8,12},{9,13},{10,... | collective-permute-start | bytes 442376 | tf_op jit(solution)/shard_map/ppermute | solution.py:250
  8.6 12.8 %collective-permute-start.5 = (bf16[144,512]{1,0:T(8,128)(2,1)S(1)}, bf16[144,512]{1,0:T(8,128)(2,1)S(1)}, u32[]{:S(2)}, u32[]{:S(2)}) collective-permute-start(bf16[144,512]{1,0:T(8,128)(2,1)S(1)} %prepare.1.refs_0_), channel_id=1, source_target_pairs={{0,6},{1,7},{2,4},{3,5},{4,2},{5,3},{6,0},{7,1},{8,14},{9,15},{10,... | collective-permute-start | bytes 442376 | tf_op jit(solution)/shard_map/ppermute | solution.py:250
  17.9 2.0 %copy-start = (bf16[4096,512]{1,0:T(8,128)(2,1)}, bf16[4096,512]{1,0:T(8,128)(2,1)S(1)}, u32[]{:S(2)}) copy-start(bf16[4096,512]{1,0:T(8,128)(2,1)S(1)} %unit_gallery.1.unit_ref) | copy-start | bytes 12582916
  19.8 6.6 %collective-permute-start.4 = (bf16[144,512]{1,0:T(8,128)(2,1)S(1)}, bf16[144,512]{1,0:T(8,128)(2,1)S(1)}, u32[]{:S(2)}, u32[]{:S(2)}) collective-permute-start(bf16[144,512]{1,0:T(8,128)(2,1)S(1)} %collective-permute-done.3.refs_0_.refs_4_), channel_id=1, source_target_pairs={{0,1},{1,0},{2,3},{3,2},{4,5},{5,4},{6,7},{7,6},{8,9},{9,8},{10,11... | collective-permute-start | bytes 442376 | tf_op jit(solution)/shard_map/ppermute | solution.py:250
  21.5 6.6 %collective-permute-start.6 = (bf16[144,512]{1,0:T(8,128)(2,1)S(1)}, bf16[144,512]{1,0:T(8,128)(2,1)S(1)}, u32[]{:S(2)}, u32[]{:S(2)}) collective-permute-start(bf16[144,512]{1,0:T(8,128)(2,1)S(1)} %collective-permute-done.5.refs_1_.refs_6_), channel_id=1, source_target_pairs={{0,1},{1,0},{2,3},{3,2},{4,5},{5,4},{6,7},{7,6},{8,9},{9,8},{10,11... | collective-permute-start | bytes 442376 | tf_op jit(solution)/shard_map/ppermute | solution.py:250
  21.8 2.2 %copy-start.1 = (bf16[4096,512]{1,0:T(8,128)(2,1)S(1)}, bf16[4096,512]{1,0:T(8,128)(2,1)}, u32[]{:S(2)}) copy-start(bf16[4096,512]{1,0:T(8,128)(2,1)} %copy-done) | copy-start | bytes 12582916
  24.0 5.5 %copy-start.2 = (bf16[4096,512]{1,0:T(8,128)(2,1)S(1)}, bf16[4096,512]{1,0:T(8,128)(2,1)}, u32[]{:S(2)}) copy-start(bf16[4096,512]{1,0:T(8,128)(2,1)} %copy-done) | copy-start | bytes 12582916
  28.1 5.0 %collective-permute-start.8 = (bf16[128,512]{1,0:T(8,128)(2,1)S(1)}, bf16[128,512]{1,0:T(8,128)(2,1)S(1)}, u32[]{:S(2)}, u32[]{:S(2)}) collective-permute-start(bf16[128,512]{1,0:T(8,128)(2,1)S(1)} %gather_tests.1.refs_0_), channel_id=1, source_target_pairs={{0,16},{8,24},{16,0},{24,8},{1,17},{9,25},{17,1},{25,9},{2,18},{10... | collective-permute-start | bytes 393224 | tf_op jit(solution)/shard_map/ppermute | solution.py:250
  30.9 1.2 %collective-permute-start.9 = (f32[2,1024]{1,0:T(2,128)S(1)}, f32[2,1024]{1,0:T(2,128)S(1)}, u32[]{:S(2)}, u32[]{:S(2)}) collective-permute-start(f32[2,1024]{1,0:T(2,128)S(1)} %get-tuple-element.16), channel_id=1, source_target_pairs={{0,8},{8,0},{16,24},{24,16},{1,9},{9,1},{17,25},{25,17},{2,10},{10... | collective-permute-start | bytes 24584 | tf_op jit(solution)/shard_map/ppermute | solution.py:250
  31.0 3.7 %collective-permute-start.7 = (bf16[128,512]{1,0:T(8,128)(2,1)S(1)}, bf16[128,512]{1,0:T(8,128)(2,1)S(1)}, u32[]{:S(2)}, u32[]{:S(2)}) collective-permute-start(bf16[128,512]{1,0:T(8,128)(2,1)S(1)} %gather_tests.1.refs_0_), channel_id=1, source_target_pairs={{0,8},{8,0},{16,24},{24,16},{1,9},{9,1},{17,25},{25,17},{2,10},{10... | collective-permute-start | bytes 393224 | tf_op jit(solution)/shard_map/ppermute | solution.py:250
  33.1 1.5 %collective-permute-start.10 = (bf16[128,512]{1,0:T(8,128)(2,1)S(1)}, bf16[128,512]{1,0:T(8,128)(2,1)S(1)}, u32[]{:S(2)}, u32[]{:S(2)}) collective-permute-start(bf16[128,512]{1,0:T(8,128)(2,1)S(1)} %collective-permute-done.8.refs_2_), channel_id=1, source_target_pairs={{0,8},{8,0},{16,24},{24,16},{1,9},{9,1},{17,25},{25,17},{2,10},{10... | collective-permute-start | bytes 393224 | tf_op jit(solution)/shard_map/ppermute | solution.py:250
  33.1 3.7 %collective-permute-start.11 = (f32[1,1024]{1,0:T(1,128)S(1)}, f32[1,1024]{1,0:T(1,128)S(1)}, u32[]{:S(2)}, u32[]{:S(2)}) collective-permute-start(f32[1,1024]{1,0:T(1,128)S(1)} %slice_add_fusion), channel_id=1, source_target_pairs={{0,16},{8,24},{16,0},{24,8},{1,17},{9,25},{17,1},{25,9},{2,18},{10... | collective-permute-start | bytes 12296 | tf_op jit(solution)/shard_map/ppermute | solution.py:250

commit v3 on v2

--- a/solution.py
+++ b/solution.py
@@ -79,6 +79,23 @@
     )
 
 
+def normalize(captions):
+    rows, width = captions.shape
+
+    def kernel(captions_ref, out_ref):
+        out_ref[...] = unit_rows(captions_ref[...])
+
+    return call(
+        kernel,
+        "normalize",
+        jax.ShapeDtypeStruct((rows, width), jnp.bfloat16),
+        10**9,
+        4 * rows * width,
+        captions,
+        in_specs=[in_vmem],
+    )
+
+
 def unit_gallery(bank, gallery, share):
     clips, width = gallery.shape
     quarters = clips // share
@@ -112,12 +129,17 @@
     )
 
 
-def first_sums(unit, payloads, rows):
+def first_sums(unit, payloads, raw, rows):
     clips, width = unit.shape
+    done = len(payloads)
+    payloads = payloads + raw
     count = len(payloads)
 
     def kernel(unit_ref, *refs):
-        captions = jnp.concatenate([ref[:rows, :] for ref in refs[:count]], axis=0)
+        captions = jnp.concatenate(
+            [ref[:rows, :] for ref in refs[:done]] + [unit_rows(ref[...]) for ref in refs[done:count]],
+            axis=0,
+        )
         refs[count][...] = exp_sums(captions, unit_ref[...])
 
     return call(
@@ -132,13 +154,13 @@
     )
 
 
-def last_sums(unit, payloads, sums, rows, share):
+def last_sums(unit, raw, sums, rows, share):
     clips, width = unit.shape
-    count, parts = len(payloads), len(sums)
+    count, parts = len(raw), len(sums)
     half = clips // share // 2
 
     def kernel(unit_ref, *refs):
-        captions = jnp.concatenate([ref[:rows, :] for ref in refs[:count]], axis=0)
+        captions = jnp.concatenate([ref[...] for ref in refs[:count]], axis=0)
         total = exp_sums(captions, unit_ref[...])
         for ref in refs[count : count + parts]:
             total = total + ref[...]
@@ -155,31 +177,52 @@
         2 * rows * clips * width * count,
         2 * clips * width,
         unit,
-        *payloads,
+        *raw,
         *sums,
         in_specs=[in_vmem] * (1 + count + parts),
         out_specs=[in_vmem] * 2,
     )
 
 
-def gather_tests(gal, payloads, rows):
+def near_tests(gal, payloads, rows):
     total, width = payloads[0].shape
     more, count = total - rows, len(payloads)
 
     def kernel(gal_ref, *refs):
         for mask in range(count):
-            place = pl.multiple_of((gal_ref[0] ^ mask) * more, more)
+            place = pl.multiple_of(((gal_ref[0] ^ mask) % count) * more, more)
             refs[count][pl.ds(place, more), :] = refs[mask][rows:, :]
 
     return call(
         kernel,
-        "gather_tests",
+        "near_tests",
         jax.ShapeDtypeStruct((count * more, width), jnp.bfloat16),
         0,
         4 * count * more * width,
         gal,
         *payloads,
         in_specs=[in_smem] + [in_vmem] * count,
+    )
+
+
+def all_tests(gal, near, far, near_count):
+    rows, width = near.shape
+
+    def kernel(gal_ref, near_ref, far_ref, out_ref):
+        half = (gal_ref[0] // near_count) % 2
+        out_ref[pl.ds(pl.multiple_of(half * rows, rows), rows), :] = near_ref[...]
+        out_ref[pl.ds(pl.multiple_of((1 - half) * rows, rows), rows), :] = far_ref[...]
+
+    return call(
+        kernel,
+        "all_tests",
+        jax.ShapeDtypeStruct((2 * rows, width), jnp.bfloat16),
+        0,
+        8 * rows * width,
+        gal,
+        near,
+        far,
+        in_specs=[in_smem] + [in_vmem] * 2,
     )
 
 
@@ -261,36 +304,27 @@
     bank = lax.axis_index("bank").astype(jnp.int32)[None]
     gal = lax.axis_index("gal").astype(jnp.int32)[None]
 
+    half = shards // 2
+    across = normalize(swap(querybank, "gal", half))
     payload = prepare(querybank, test_queries)
-    low = shards // 4
-    got = {0: payload}
-    for high in (2, 3, 1):
-        got[high * low] = swap(payload, "gal", high * low)
-    for mask in range(1, low):
-        got[low + mask] = swap(payload, "gal", low + mask)
-        got[mask] = swap(payload, "gal", mask)
+    near = [payload] + [swap(payload, "gal", mask) for mask in range(1, half)]
 
     unit = unit_gallery(bank, gallery, share)
-    sums = [first_sums(unit, [got[m] for m in range(2 * low)], rows)]
-    for high in (2, 3):
-        here = after(got[high * low], sums[0])
-        for mask in range(1, low):
-            got[high * low + mask] = swap(here, "gal", mask)
-    sums.append(first_sums(unit, [got[2 * low], got[3 * low]], rows))
-
-    for high in (2, 3):
-        for mask in range(1, low):
-            got[high * low + mask] = after(got[high * low + mask], sums[1])
-    tests = gather_tests(gal, [got[m] for m in range(shards)], rows)
+    here = near_tests(gal, [near[0]] + [after(x, across) for x in near[1:]], rows)
+    there = swap(here, "gal", half)
+    last = [swap(across, "gal", mask) for mask in range(1, half)]
+    sums = [first_sums(unit, near, [], rows)]
+
+    tests = all_tests(gal, here, there, half)
     tests_y = swap(tests, "bank", 2)
     tests_core = swap(tests, "bank", 1)
-    last = [got[h * low + m] for h in (2, 3) for m in range(1, low)]
-    keep, send = last_sums(unit, last, sums, rows, share)
+    tests_both = swap(tests_y, "bank", 1)
+    raw = raw_scores(unit, [tests, tests_core, tests_y, tests_both], share)
+
+    keep, send = last_sums(unit, [across] + last, sums, rows, share)
     received = swap(send, "bank", 1)
-    far = swap(keep[1:] + received[1:], "bank", 2)
-    tests_both = swap(after(tests_y, received), "bank", 1)
-    raw = raw_scores(unit, [tests, tests_core, tests_y, tests_both], share)
-    result = write_scores(bank, raw, keep, received, far, groups, rows * shards * groups)
+    other = swap(keep[1:] + received[1:], "bank", 2)
+    result = write_scores(bank, raw, keep, received, other, groups, rows * shards * groups)
     return result.reshape(-1, 1, share)
 
 

time: 38.5 us -> 33 us (0.86)
  local copies, waits for them, and re-layouts: 4.14 us -> 0 us
  waiting for transfers between devices: 8.67 us -> 6.37 us
  starting transfers between devices: 14.6 us -> 15.6 us
    unnamed x6 -> x0, local copies, waits for them, and re-layouts: 4.14 us -> none
    ppermute x12 -> x13, waiting for transfers between devices: 8.67 us -> 6.37 us  [swap(): return lax.ppermute(values, axis, [(i, i ^ mask) for i in range(size)])]
    ppermute x12 -> x13, starting transfers between devices: 14.6 us -> 15.6 us  [swap(): return lax.ppermute(values, axis, [(i, i ^ mask) for i in range(size)])]
    pallas_call x8 -> x9, Pallas kernels: 10.8 us -> 10.8 us  [call(): pl.pallas_call(kernel, out_shape=out_shape, in_specs=in_specs, out_specs=...]
  transfers between devices with their start and end apart: 12 -> 13, of which waited for: 7 -> 5; matrix products, arithmetic and copies ran while one was open for 0% -> 0% of each run, Pallas kernels for 22% -> 28%
where the time goes in v3:
time: 33 us; the launch traced here: 32.8 us
  starting transfers between devices  15.6 us (47%)
  Pallas kernels  10.8 us (33%)
  waiting for transfers between devices  6.37 us (19%)
    ppermute x13, starting transfers between devices, swap(): return lax.ppermute(values, axis, [(i, i ^ mask) for i in range(size)])  15.6 us
    pallas_call x9, Pallas kernels, call(): pl.pallas_call(kernel, out_shape=out_shape, in_specs=in_specs, out_specs=...  10.8 us
    ppermute x13, waiting for transfers between devices, swap(): return lax.ppermute(values, axis, [(i, i ^ mask) for i in range(size)])  6.37 us
  transfers between devices with their start and end apart: 13, of which 5 were waited for; matrix products, arithmetic and copies ran while one was open for 0% of the time, Pallas kernels for 28%

profile of v3, /device:TPU:0, one launch (start us, length us, event | category | flops | bytes accessed | tf_op | source)
XLA Modules:
  0.0 32.8 jit_solution(4616931079519986572)
XLA Ops:
  0.0 4.0 %collective-permute-start.1 = (bf16[128,512]{1,0:T(8,128)(2,1)}, bf16[128,512]{1,0:T(8,128)(2,1)S(1)}, u32[]{:S(2)}, u32[]{:S(2)}) collective-permute-start(bf16[128,512]{1,0:T(8,128)(2,1)} %captions_ref.1), channel_id=1, source_target_pairs={{0,4},{1,5},{2,6},{3,7},{4,0},{5,1},{6,2},{7,3},{8,12},{9,13},{10,... | collective-permute-start | bytes 393224 | tf_op jit(solution)/shard_map/ppermute | solution.py:293
  4.0 1.1 %prepare.1.refs_0_ = bf16[144,512]{1,0:T(8,128)(2,1)S(1)} custom-call(bf16[128,512]{1,0:T(8,128)(2,1)} %captions_ref.1, bf16[16,512]{1,0:T(8,128)(2,1)} %tests_ref.1), custom_call_target="tpu_custom_call" | custom-call | flops 65536 | bytes 262144 | tf_op jit(solution)/shard_map/prepare/pallas_call | solution.py:36
  5.1 2.6 %collective-permute-start.3 = (bf16[144,512]{1,0:T(8,128)(2,1)S(1)}, bf16[144,512]{1,0:T(8,128)(2,1)S(1)}, u32[]{:S(2)}, u32[]{:S(2)}) collective-permute-start(bf16[144,512]{1,0:T(8,128)(2,1)S(1)} %prepare.1.refs_0_), channel_id=1, source_target_pairs={{0,3},{1,2},{2,1},{3,0},{4,7},{5,6},{6,5},{7,4},{8,11},{9,10},{10,... | collective-permute-start | bytes 442376 | tf_op jit(solution)/shard_map/ppermute | solution.py:293
  7.7 0.4 %collective-permute-start.2 = (bf16[144,512]{1,0:T(8,128)(2,1)S(1)}, bf16[144,512]{1,0:T(8,128)(2,1)S(1)}, u32[]{:S(2)}, u32[]{:S(2)}) collective-permute-start(bf16[144,512]{1,0:T(8,128)(2,1)S(1)} %prepare.1.refs_0_), channel_id=1, source_target_pairs={{0,2},{1,3},{2,0},{3,1},{4,6},{5,7},{6,4},{7,5},{8,10},{9,11},{10,... | collective-permute-start | bytes 442376 | tf_op jit(solution)/shard_map/ppermute | solution.py:293
  8.1 0.5 %collective-permute-start = (bf16[144,512]{1,0:T(8,128)(2,1)S(1)}, bf16[144,512]{1,0:T(8,128)(2,1)S(1)}, u32[]{:S(2)}, u32[]{:S(2)}) collective-permute-start(bf16[144,512]{1,0:T(8,128)(2,1)S(1)} %prepare.1.refs_0_), channel_id=1, source_target_pairs={{0,1},{1,0},{2,3},{3,2},{4,5},{5,4},{6,7},{7,6},{8,9},{9,8},{10,11... | collective-permute-start | bytes 442376 | tf_op jit(solution)/shard_map/ppermute | solution.py:293
  8.7 2.6 %unit_gallery.1.unit_ref = bf16[4096,512]{1,0:T(8,128)(2,1)S(1)} custom-call(s32[1]{0:T(128)} %bitcast.bank_ref, bf16[4096,512]{1,0:T(8,128)(2,1)} %gallery_ref.1), custom_call_target="tpu_custom_call" | custom-call | flops 8388608 | bytes 8388608 | tf_op jit(solution)/shard_map/unit_gallery/pallas_call | solution.py:36
  11.2 0.0 collective-permute-done.1.captions_ref
  11.3 0.1 normalize.1.refs_0_
  11.4 2.6 %collective-permute-start.10 = (bf16[128,512]{1,0:T(8,128)(2,1)S(1)}, bf16[128,512]{1,0:T(8,128)(2,1)S(1)}, u32[]{:S(2)}, u32[]{:S(2)}) collective-permute-start(bf16[128,512]{1,0:T(8,128)(2,1)S(1)} %normalize.1.refs_0_), channel_id=1, source_target_pairs={{0,3},{1,2},{2,1},{3,0},{4,7},{5,6},{6,5},{7,4},{8,11},{9,10},{10,... | collective-permute-start | bytes 393224 | tf_op jit(solution)/shard_map/ppermute | solution.py:293
  13.9 0.4 %collective-permute-start.9 = (bf16[128,512]{1,0:T(8,128)(2,1)S(1)}, bf16[128,512]{1,0:T(8,128)(2,1)S(1)}, u32[]{:S(2)}, u32[]{:S(2)}) collective-permute-start(bf16[128,512]{1,0:T(8,128)(2,1)S(1)} %normalize.1.refs_0_), channel_id=1, source_target_pairs={{0,2},{1,3},{2,0},{3,1},{4,6},{5,7},{6,4},{7,5},{8,10},{9,11},{10,... | collective-permute-start | bytes 393224 | tf_op jit(solution)/shard_map/ppermute | solution.py:293
  14.4 0.0 collective-permute-done.3.refs_3_
  14.4 0.9 %collective-permute-start.8 = (bf16[128,512]{1,0:T(8,128)(2,1)S(1)}, bf16[128,512]{1,0:T(8,128)(2,1)S(1)}, u32[]{:S(2)}, u32[]{:S(2)}) collective-permute-start(bf16[128,512]{1,0:T(8,128)(2,1)S(1)} %normalize.1.refs_0_), channel_id=1, source_target_pairs={{0,1},{1,0},{2,3},{3,2},{4,5},{5,4},{6,7},{7,6},{8,9},{9,8},{10,11... | collective-permute-start | bytes 393224 | tf_op jit(solution)/shard_map/ppermute | solution.py:293
  15.3 1.7 %collective-permute-done.2.refs_2_ = bf16[144,512]{1,0:T(8,128)(2,1)S(1)} collective-permute-done((bf16[144,512]{1,0:T(8,128)(2,1)S(1)}, bf16[144,512]{1,0:T(8,128)(2,1)S(1)}, u32[]{:S(2)}, u32[]{:S(2)}) %collective-permute-start.2) | collective-permute-done | bytes 147488 | tf_op jit(solution)/shard_map/ppermute | solution.py:293
  16.9 0.0 collective-permute-done.refs_1_
  17.0 0.5 %collective-permute-start.4 = (bf16[64,512]{1,0:T(8,128)(2,1)S(1)}, bf16[64,512]{1,0:T(8,128)(2,1)S(1)}, u32[]{:S(2)}, u32[]{:S(2)}) collective-permute-start(bf16[64,512]{1,0:T(8,128)(2,1)S(1)} %near_tests.1.near_ref), channel_id=1, source_target_pairs={{0,4},{1,5},{2,6},{3,7},{4,0},{5,1},{6,2},{7,3},{8,12},{9,13},{10,... | collective-permute-start | bytes 196616 | tf_op jit(solution)/shard_map/ppermute | solution.py:293
  17.5 2.4 %first_sums.1.refs_4_ = f32[8,4096]{1,0:T(8,128)S(1)} custom-call(bf16[4096,512]{1,0:T(8,128)(2,1)S(1)} %unit_gallery.1.unit_ref, bf16[144,512]{1,0:T(8,128)(2,1)S(1)} %prepare.1.refs_0_, bf16[144,512]{1,0:T(8,128)(2,1)S(1)} %collective-permute-done.refs_1_, bf16[144,512]{1,0:T(8,128)(2,1)S(1)} %collective-permute-done.2.refs_2_, ...), custom_call_target="tpu_custom_call" | custom-call | flops 2147483648 | bytes 4194304 | tf_op jit(solution)/shard_map/first_sums/pallas_call | solution.py:36
  19.9 2.5 %collective-permute-done.4.far_ref = bf16[64,512]{1,0:T(8,128)(2,1)S(1)} collective-permute-done((bf16[64,512]{1,0:T(8,128)(2,1)S(1)}, bf16[64,512]{1,0:T(8,128)(2,1)S(1)}, u32[]{:S(2)}, u32[]{:S(2)}) %collective-permute-start.4) | collective-permute-done | bytes 65568 | tf_op jit(solution)/shard_map/ppermute | solution.py:293
  22.4 1.6 %collective-permute-start.6 = (bf16[128,512]{1,0:T(8,128)(2,1)S(1)}, bf16[128,512]{1,0:T(8,128)(2,1)S(1)}, u32[]{:S(2)}, u32[]{:S(2)}) collective-permute-start(bf16[128,512]{1,0:T(8,128)(2,1)S(1)} %all_tests.1.refs_0_), channel_id=1, source_target_pairs={{0,16},{8,24},{16,0},{24,8},{1,17},{9,25},{17,1},{25,9},{2,18},{10... | collective-permute-start | bytes 393224 | tf_op jit(solution)/shard_map/ppermute | solution.py:293
  24.0 0.0 collective-permute-done.10.refs_3_
  24.0 0.0 collective-permute-done.9.refs_2_
  24.0 0.0 collective-permute-done.8.refs_1_
  24.0 2.4 %last_sums.1 = (f32[2,1024]{1,0:T(2,128)S(1)}, f32[2,1024]{1,0:T(2,128)S(1)}) custom-call(bf16[4096,512]{1,0:T(8,128)(2,1)S(1)} %unit_gallery.1.unit_ref, bf16[128,512]{1,0:T(8,128)(2,1)S(1)} %normalize.1.refs_0_, bf16[128,512]{1,0:T(8,128)(2,1)S(1)} %collective-permute-done.8.refs_1_, bf16[128,512]{1,0:T(8,128)(2,1)S(1)} %collective-permute-done.9.refs_2_, ...), custom_call_target="tpu_custom_call" | custom-call | flops 2147483648 | bytes 4194304 | tf_op jit(solution)/shard_map/last_sums/pallas_call | solution.py:36
  26.4 0.1 collective-permute-start.11
  26.4 0.5 %collective-permute-start.5 = (bf16[128,512]{1,0:T(8,128)(2,1)S(1)}, bf16[128,512]{1,0:T(8,128)(2,1)S(1)}, u32[]{:S(2)}, u32[]{:S(2)}) collective-permute-start(bf16[128,512]{1,0:T(8,128)(2,1)S(1)} %all_tests.1.refs_0_), channel_id=1, source_target_pairs={{0,8},{8,0},{16,24},{24,16},{1,9},{9,1},{17,25},{25,17},{2,10},{10... | collective-permute-start | bytes 393224 | tf_op jit(solution)/shard_map/ppermute | solution.py:293
  26.9 0.5 %collective-permute-done.6.refs_2_ = bf16[128,512]{1,0:T(8,128)(2,1)S(1)} collective-permute-done((bf16[128,512]{1,0:T(8,128)(2,1)S(1)}, bf16[128,512]{1,0:T(8,128)(2,1)S(1)}, u32[]{:S(2)}, u32[]{:S(2)}) %collective-permute-start.6) | collective-permute-done | bytes 131104 | tf_op jit(solution)/shard_map/ppermute | solution.py:293
  27.4 0.0 collective-permute-start.7
  27.4 0.2 collective-permute-done.11.received_ref
  27.6 1.4 %collective-permute-start.12 = (f32[1,1024]{1,0:T(1,128)S(1)}, f32[1,1024]{1,0:T(1,128)S(1)}, u32[]{:S(2)}, u32[]{:S(2)}) collective-permute-start(f32[1,1024]{1,0:T(1,128)S(1)} %slice_add_fusion), channel_id=1, source_target_pairs={{0,16},{8,24},{16,0},{24,8},{1,17},{9,25},{17,1},{25,9},{2,18},{10... | collective-permute-start | bytes 12296 | tf_op jit(solution)/shard_map/ppermute | solution.py:293
  29.0 0.0 collective-permute-done.5.refs_1_
  29.0 0.7 %raw_scores.1.raw_ref = f32[512,1024]{1,0:T(8,128)S(1)} custom-call(bf16[4096,512]{1,0:T(8,128)(2,1)S(1)} %unit_gallery.1.unit_ref, bf16[128,512]{1,0:T(8,128)(2,1)S(1)} %all_tests.1.refs_0_, bf16[128,512]{1,0:T(8,128)(2,1)S(1)} %collective-permute-done.5.refs_1_, bf16[128,512]{1,0:T(8,128)(2,1)S(1)} %collective-permute-done.6.refs_2_, ...), custom_call_target="tpu_custom_call" | custom-call | flops 536870912 | bytes 2097152 | tf_op jit(solution)/shard_map/raw_scores/pallas_call | solution.py:36
  29.8 1.5 %collective-permute-done.12.far_ref = f32[1,1024]{1,0:T(1,128)S(1)} collective-permute-done((f32[1,1024]{1,0:T(1,128)S(1)}, f32[1,1024]{1,0:T(1,128)S(1)}, u32[]{:S(2)}, u32[]{:S(2)}) %collective-permute-start.12) | collective-permute-done | bytes 4128 | tf_op jit(solution)/shard_map/ppermute | solution.py:293
  31.3 1.5 %write_scores.1 = f32[4096,128]{1,0:T(8,128)} custom-call(s32[1]{0:T(128)} %bitcast.bank_ref, f32[512,1024]{1,0:T(8,128)S(1)} %raw_scores.1.raw_ref, f32[2,1024]{1,0:T(2,128)S(1)} %get-tuple-element.13.keep_ref, f32[2,1024]{1,0:T(2,128)S(1)} %collective-permute-done.11.received_ref, f32[1,1024]{1,0:T(1,128)S(1)} %collective-permute-done.12.far_ref), custom_call_target="tpu_custom_call" | custom-call | flops 524288 | bytes 4194304 | tf_op jit(solution)/shard_map/write_scores/pallas_call | solution.py:36
  (4 shorter events, 0.0 us)
Async XLA Ops:
  0.0 11.2 %collective-permute-start.1 = (bf16[128,512]{1,0:T(8,128)(2,1)}, bf16[128,512]{1,0:T(8,128)(2,1)S(1)}, u32[]{:S(2)}, u32[]{:S(2)}) collective-permute-start(bf16[128,512]{1,0:T(8,128)(2,1)} %captions_ref.1), channel_id=1, source_target_pairs={{0,4},{1,5},{2,6},{3,7},{4,0},{5,1},{6,2},{7,3},{8,12},{9,13},{10,... | collective-permute-start | bytes 393224 | tf_op jit(solution)/shard_map/ppermute | solution.py:293
  5.1 9.3 %collective-permute-start.3 = (bf16[144,512]{1,0:T(8,128)(2,1)S(1)}, bf16[144,512]{1,0:T(8,128)(2,1)S(1)}, u32[]{:S(2)}, u32[]{:S(2)}) collective-permute-start(bf16[144,512]{1,0:T(8,128)(2,1)S(1)} %prepare.1.refs_0_), channel_id=1, source_target_pairs={{0,3},{1,2},{2,1},{3,0},{4,7},{5,6},{6,5},{7,4},{8,11},{9,10},{10,... | collective-permute-start | bytes 442376 | tf_op jit(solution)/shard_map/ppermute | solution.py:293
  7.7 9.3 %collective-permute-start.2 = (bf16[144,512]{1,0:T(8,128)(2,1)S(1)}, bf16[144,512]{1,0:T(8,128)(2,1)S(1)}, u32[]{:S(2)}, u32[]{:S(2)}) collective-permute-start(bf16[144,512]{1,0:T(8,128)(2,1)S(1)} %prepare.1.refs_0_), channel_id=1, source_target_pairs={{0,2},{1,3},{2,0},{3,1},{4,6},{5,7},{6,4},{7,5},{8,10},{9,11},{10,... | collective-permute-start | bytes 442376 | tf_op jit(solution)/shard_map/ppermute | solution.py:293
  8.1 8.8 %collective-permute-start = (bf16[144,512]{1,0:T(8,128)(2,1)S(1)}, bf16[144,512]{1,0:T(8,128)(2,1)S(1)}, u32[]{:S(2)}, u32[]{:S(2)}) collective-permute-start(bf16[144,512]{1,0:T(8,128)(2,1)S(1)} %prepare.1.refs_0_), channel_id=1, source_target_pairs={{0,1},{1,0},{2,3},{3,2},{4,5},{5,4},{6,7},{7,6},{8,9},{9,8},{10,11... | collective-permute-start | bytes 442376 | tf_op jit(solution)/shard_map/ppermute | solution.py:293
  11.4 12.6 %collective-permute-start.10 = (bf16[128,512]{1,0:T(8,128)(2,1)S(1)}, bf16[128,512]{1,0:T(8,128)(2,1)S(1)}, u32[]{:S(2)}, u32[]{:S(2)}) collective-permute-start(bf16[128,512]{1,0:T(8,128)(2,1)S(1)} %normalize.1.refs_0_), channel_id=1, source_target_pairs={{0,3},{1,2},{2,1},{3,0},{4,7},{5,6},{6,5},{7,4},{8,11},{9,10},{10,... | collective-permute-start | bytes 393224 | tf_op jit(solution)/shard_map/ppermute | solution.py:293
  13.9 10.0 %collective-permute-start.9 = (bf16[128,512]{1,0:T(8,128)(2,1)S(1)}, bf16[128,512]{1,0:T(8,128)(2,1)S(1)}, u32[]{:S(2)}, u32[]{:S(2)}) collective-permute-start(bf16[128,512]{1,0:T(8,128)(2,1)S(1)} %normalize.1.refs_0_), channel_id=1, source_target_pairs={{0,2},{1,3},{2,0},{3,1},{4,6},{5,7},{6,4},{7,5},{8,10},{9,11},{10,... | collective-permute-start | bytes 393224 | tf_op jit(solution)/shard_map/ppermute | solution.py:293
  14.4 9.6 %collective-permute-start.8 = (bf16[128,512]{1,0:T(8,128)(2,1)S(1)}, bf16[128,512]{1,0:T(8,128)(2,1)S(1)}, u32[]{:S(2)}, u32[]{:S(2)}) collective-permute-start(bf16[128,512]{1,0:T(8,128)(2,1)S(1)} %normalize.1.refs_0_), channel_id=1, source_target_pairs={{0,1},{1,0},{2,3},{3,2},{4,5},{5,4},{6,7},{7,6},{8,9},{9,8},{10,11... | collective-permute-start | bytes 393224 | tf_op jit(solution)/shard_map/ppermute | solution.py:293
  17.0 5.4 %collective-permute-start.4 = (bf16[64,512]{1,0:T(8,128)(2,1)S(1)}, bf16[64,512]{1,0:T(8,128)(2,1)S(1)}, u32[]{:S(2)}, u32[]{:S(2)}) collective-permute-start(bf16[64,512]{1,0:T(8,128)(2,1)S(1)} %near_tests.1.near_ref), channel_id=1, source_target_pairs={{0,4},{1,5},{2,6},{3,7},{4,0},{5,1},{6,2},{7,3},{8,12},{9,13},{10,... | collective-permute-start | bytes 196616 | tf_op jit(solution)/shard_map/ppermute | solution.py:293
  22.4 5.0 %collective-permute-start.6 = (bf16[128,512]{1,0:T(8,128)(2,1)S(1)}, bf16[128,512]{1,0:T(8,128)(2,1)S(1)}, u32[]{:S(2)}, u32[]{:S(2)}) collective-permute-start(bf16[128,512]{1,0:T(8,128)(2,1)S(1)} %all_tests.1.refs_0_), channel_id=1, source_target_pairs={{0,16},{8,24},{16,0},{24,8},{1,17},{9,25},{17,1},{25,9},{2,18},{10... | collective-permute-start | bytes 393224 | tf_op jit(solution)/shard_map/ppermute | solution.py:293
  26.4 1.2 %collective-permute-start.11 = (f32[2,1024]{1,0:T(2,128)S(1)}, f32[2,1024]{1,0:T(2,128)S(1)}, u32[]{:S(2)}, u32[]{:S(2)}) collective-permute-start(f32[2,1024]{1,0:T(2,128)S(1)} %get-tuple-element.14), channel_id=1, source_target_pairs={{0,8},{8,0},{16,24},{24,16},{1,9},{9,1},{17,25},{25,17},{2,10},{10... | collective-permute-start | bytes 24584 | tf_op jit(solution)/shard_map/ppermute | solution.py:293
  26.4 2.6 %collective-permute-start.5 = (bf16[128,512]{1,0:T(8,128)(2,1)S(1)}, bf16[128,512]{1,0:T(8,128)(2,1)S(1)}, u32[]{:S(2)}, u32[]{:S(2)}) collective-permute-start(bf16[128,512]{1,0:T(8,128)(2,1)S(1)} %all_tests.1.refs_0_), channel_id=1, source_target_pairs={{0,8},{8,0},{16,24},{24,16},{1,9},{9,1},{17,25},{25,17},{2,10},{10... | collective-permute-start | bytes 393224 | tf_op jit(solution)/shard_map/ppermute | solution.py:293
  27.4 1.6 %collective-permute-start.7 = (bf16[128,512]{1,0:T(8,128)(2,1)S(1)}, bf16[128,512]{1,0:T(8,128)(2,1)S(1)}, u32[]{:S(2)}, u32[]{:S(2)}) collective-permute-start(bf16[128,512]{1,0:T(8,128)(2,1)S(1)} %collective-permute-done.6.refs_2_), channel_id=1, source_target_pairs={{0,8},{8,0},{16,24},{24,16},{1,9},{9,1},{17,25},{25,17},{2,10},{10... | collective-permute-start | bytes 393224 | tf_op jit(solution)/shard_map/ppermute | solution.py:293
  27.6 3.7 %collective-permute-start.12 = (f32[1,1024]{1,0:T(1,128)S(1)}, f32[1,1024]{1,0:T(1,128)S(1)}, u32[]{:S(2)}, u32[]{:S(2)}) collective-permute-start(f32[1,1024]{1,0:T(1,128)S(1)} %slice_add_fusion), channel_id=1, source_target_pairs={{0,16},{8,24},{16,0},{24,8},{1,17},{9,25},{17,1},{25,9},{2,18},{10... | collective-permute-start | bytes 12296 | tf_op jit(solution)/shard_map/ppermute | solution.py:293

commit v4 on v3

--- a/solution.py
+++ b/solution.py
@@ -167,8 +167,8 @@
         total = jnp.sum(total, axis=0, keepdims=True)
         keep_ref, send_ref = refs[count + parts :]
         for k in range(half):
-            keep_ref[k : k + 1, :] = total[:, 2 * k * share : (2 * k + 1) * share]
-            send_ref[k : k + 1, :] = total[:, (2 * k + 1) * share : (2 * k + 2) * share]
+            keep_ref[k : k + 1, :] = total[:, k * share : (k + 1) * share]
+            send_ref[k : k + 1, :] = total[:, (half + k) * share : (half + k + 1) * share]
 
     return call(
         kernel,
@@ -315,15 +315,16 @@
     last = [swap(across, "gal", mask) for mask in range(1, half)]
     sums = [first_sums(unit, near, [], rows)]
 
-    tests = all_tests(gal, here, there, half)
+    sums.append(first_sums(unit, [across, last[0]], [], rows))
+    tests = all_tests(gal, here, after(there, sums), half)
     tests_y = swap(tests, "bank", 2)
     tests_core = swap(tests, "bank", 1)
     tests_both = swap(tests_y, "bank", 1)
     raw = raw_scores(unit, [tests, tests_core, tests_y, tests_both], share)
 
-    keep, send = last_sums(unit, [across] + last, sums, rows, share)
-    received = swap(send, "bank", 1)
-    other = swap(keep[1:] + received[1:], "bank", 2)
+    keep, send = last_sums(unit, [after(last[1], tests), after(last[2], tests)], sums, rows, share)
+    received = swap(send, "bank", 2)
+    other = swap(keep[1:] + received[1:], "bank", 1)
     result = write_scores(bank, raw, keep, received, other, groups, rows * shards * groups)
     return result.reshape(-1, 1, share)
 

time: 33 us -> 32 us (0.970)
  starting transfers between devices: 15.6 us -> 14.6 us
    ppermute x13, starting transfers between devices: 15.6 us -> 14.6 us  [swap(): return lax.ppermute(values, axis, [(i, i ^ mask) for i in range(size)])]
    pallas_call x9 -> x10, Pallas kernels: 10.8 us -> 11 us  [call(): pl.pallas_call(kernel, out_shape=out_shape, in_specs=in_specs, out_specs=...]
  transfers between devices with their start and end apart: 13 -> 13, of which waited for: 5 -> 6; matrix products, arithmetic and copies ran while one was open for 0% -> 0% of each run, Pallas kernels for 28% -> 30%
where the time goes in v4:
time: 32 us; the launch traced here: 31.7 us
  starting transfers between devices  14.6 us (46%)
  Pallas kernels  11 us (34%)
  waiting for transfers between devices  6.05 us (19%)
    ppermute x13, starting transfers between devices, swap(): return lax.ppermute(values, axis, [(i, i ^ mask) for i in range(size)])  14.6 us
    pallas_call x10, Pallas kernels, call(): pl.pallas_call(kernel, out_shape=out_shape, in_specs=in_specs, out_specs=...  11 us
    ppermute x13, waiting for transfers between devices, swap(): return lax.ppermute(values, axis, [(i, i ^ mask) for i in range(size)])  6.05 us
  transfers between devices with their start and end apart: 13, of which 6 were waited for; matrix products, arithmetic and copies ran while one was open for 0% of the time, Pallas kernels for 30%

profile of v4, /device:TPU:0, one launch (start us, length us, event | category | flops | bytes accessed | tf_op | source)
XLA Modules:
  0.0 31.7 jit_solution(292784041734885407)
XLA Ops:
  0.0 4.0 %collective-permute-start.1 = (bf16[128,512]{1,0:T(8,128)(2,1)}, bf16[128,512]{1,0:T(8,128)(2,1)S(1)}, u32[]{:S(2)}, u32[]{:S(2)}) collective-permute-start(bf16[128,512]{1,0:T(8,128)(2,1)} %captions_ref.1), channel_id=1, source_target_pairs={{0,4},{1,5},{2,6},{3,7},{4,0},{5,1},{6,2},{7,3},{8,12},{9,13},{10,... | collective-permute-start | bytes 393224 | tf_op jit(solution)/shard_map/ppermute | solution.py:293
  4.0 1.1 %prepare.1.refs_0_ = bf16[144,512]{1,0:T(8,128)(2,1)S(1)} custom-call(bf16[128,512]{1,0:T(8,128)(2,1)} %captions_ref.1, bf16[16,512]{1,0:T(8,128)(2,1)} %tests_ref.1), custom_call_target="tpu_custom_call" | custom-call | flops 65536 | bytes 262144 | tf_op jit(solution)/shard_map/prepare/pallas_call | solution.py:36
  5.1 2.6 %collective-permute-start.3 = (bf16[144,512]{1,0:T(8,128)(2,1)S(1)}, bf16[144,512]{1,0:T(8,128)(2,1)S(1)}, u32[]{:S(2)}, u32[]{:S(2)}) collective-permute-start(bf16[144,512]{1,0:T(8,128)(2,1)S(1)} %prepare.1.refs_0_), channel_id=1, source_target_pairs={{0,3},{1,2},{2,1},{3,0},{4,7},{5,6},{6,5},{7,4},{8,11},{9,10},{10,... | collective-permute-start | bytes 442376 | tf_op jit(solution)/shard_map/ppermute | solution.py:293
  7.7 0.4 %collective-permute-start.2 = (bf16[144,512]{1,0:T(8,128)(2,1)S(1)}, bf16[144,512]{1,0:T(8,128)(2,1)S(1)}, u32[]{:S(2)}, u32[]{:S(2)}) collective-permute-start(bf16[144,512]{1,0:T(8,128)(2,1)S(1)} %prepare.1.refs_0_), channel_id=1, source_target_pairs={{0,2},{1,3},{2,0},{3,1},{4,6},{5,7},{6,4},{7,5},{8,10},{9,11},{10,... | collective-permute-start | bytes 442376 | tf_op jit(solution)/shard_map/ppermute | solution.py:293
  8.1 0.5 %collective-permute-start = (bf16[144,512]{1,0:T(8,128)(2,1)S(1)}, bf16[144,512]{1,0:T(8,128)(2,1)S(1)}, u32[]{:S(2)}, u32[]{:S(2)}) collective-permute-start(bf16[144,512]{1,0:T(8,128)(2,1)S(1)} %prepare.1.refs_0_), channel_id=1, source_target_pairs={{0,1},{1,0},{2,3},{3,2},{4,5},{5,4},{6,7},{7,6},{8,9},{9,8},{10,11... | collective-permute-start | bytes 442376 | tf_op jit(solution)/shard_map/ppermute | solution.py:293
  8.7 2.6 %unit_gallery.1.unit_ref = bf16[4096,512]{1,0:T(8,128)(2,1)S(1)} custom-call(s32[1]{0:T(128)} %bitcast.bank_ref, bf16[4096,512]{1,0:T(8,128)(2,1)} %gallery_ref.1), custom_call_target="tpu_custom_call" | custom-call | flops 8388608 | bytes 8388608 | tf_op jit(solution)/shard_map/unit_gallery/pallas_call | solution.py:36
  11.2 0.0 collective-permute-done.1.captions_ref
  11.3 0.1 normalize.1.refs_0_
  11.4 2.6 %collective-permute-start.10 = (bf16[128,512]{1,0:T(8,128)(2,1)S(1)}, bf16[128,512]{1,0:T(8,128)(2,1)S(1)}, u32[]{:S(2)}, u32[]{:S(2)}) collective-permute-start(bf16[128,512]{1,0:T(8,128)(2,1)S(1)} %normalize.1.refs_0_), channel_id=1, source_target_pairs={{0,3},{1,2},{2,1},{3,0},{4,7},{5,6},{6,5},{7,4},{8,11},{9,10},{10,... | collective-permute-start | bytes 393224 | tf_op jit(solution)/shard_map/ppermute | solution.py:293
  13.9 0.4 %collective-permute-start.9 = (bf16[128,512]{1,0:T(8,128)(2,1)S(1)}, bf16[128,512]{1,0:T(8,128)(2,1)S(1)}, u32[]{:S(2)}, u32[]{:S(2)}) collective-permute-start(bf16[128,512]{1,0:T(8,128)(2,1)S(1)} %normalize.1.refs_0_), channel_id=1, source_target_pairs={{0,2},{1,3},{2,0},{3,1},{4,6},{5,7},{6,4},{7,5},{8,10},{9,11},{10,... | collective-permute-start | bytes 393224 | tf_op jit(solution)/shard_map/ppermute | solution.py:293
  14.4 0.0 collective-permute-done.3.refs_3_
  14.4 0.9 %collective-permute-start.5 = (bf16[128,512]{1,0:T(8,128)(2,1)S(1)}, bf16[128,512]{1,0:T(8,128)(2,1)S(1)}, u32[]{:S(2)}, u32[]{:S(2)}) collective-permute-start(bf16[128,512]{1,0:T(8,128)(2,1)S(1)} %normalize.1.refs_0_), channel_id=1, source_target_pairs={{0,1},{1,0},{2,3},{3,2},{4,5},{5,4},{6,7},{7,6},{8,9},{9,8},{10,11... | collective-permute-start | bytes 393224 | tf_op jit(solution)/shard_map/ppermute | solution.py:293
  15.3 1.7 %collective-permute-done.2.refs_2_ = bf16[144,512]{1,0:T(8,128)(2,1)S(1)} collective-permute-done((bf16[144,512]{1,0:T(8,128)(2,1)S(1)}, bf16[144,512]{1,0:T(8,128)(2,1)S(1)}, u32[]{:S(2)}, u32[]{:S(2)}) %collective-permute-start.2) | collective-permute-done | bytes 147488 | tf_op jit(solution)/shard_map/ppermute | solution.py:293
  16.9 0.0 collective-permute-done.refs_1_
  17.0 0.5 %collective-permute-start.4 = (bf16[64,512]{1,0:T(8,128)(2,1)S(1)}, bf16[64,512]{1,0:T(8,128)(2,1)S(1)}, u32[]{:S(2)}, u32[]{:S(2)}) collective-permute-start(bf16[64,512]{1,0:T(8,128)(2,1)S(1)} %near_tests.1.near_ref), channel_id=1, source_target_pairs={{0,4},{1,5},{2,6},{3,7},{4,0},{5,1},{6,2},{7,3},{8,12},{9,13},{10,... | collective-permute-start | bytes 196616 | tf_op jit(solution)/shard_map/ppermute | solution.py:293
  17.5 2.4 %first_sums.2.refs_2_ = f32[8,4096]{1,0:T(8,128)S(1)} custom-call(bf16[4096,512]{1,0:T(8,128)(2,1)S(1)} %unit_gallery.1.unit_ref, bf16[144,512]{1,0:T(8,128)(2,1)S(1)} %prepare.1.refs_0_, bf16[144,512]{1,0:T(8,128)(2,1)S(1)} %collective-permute-done.refs_1_, bf16[144,512]{1,0:T(8,128)(2,1)S(1)} %collective-permute-done.2.refs_2_, ...), custom_call_target="tpu_custom_call" | custom-call | flops 2147483648 | bytes 4194304 | tf_op jit(solution)/shard_map/first_sums/pallas_call | solution.py:36
  19.9 0.8 %collective-permute-done.5.refs_1_ = bf16[128,512]{1,0:T(8,128)(2,1)S(1)} collective-permute-done((bf16[128,512]{1,0:T(8,128)(2,1)S(1)}, bf16[128,512]{1,0:T(8,128)(2,1)S(1)}, u32[]{:S(2)}, u32[]{:S(2)}) %collective-permute-start.5) | collective-permute-done | bytes 131104 | tf_op jit(solution)/shard_map/ppermute | solution.py:293
  20.7 1.3 %first_sums.3.refs_3_ = f32[8,4096]{1,0:T(8,128)S(1)} custom-call(bf16[4096,512]{1,0:T(8,128)(2,1)S(1)} %unit_gallery.1.unit_ref, bf16[128,512]{1,0:T(8,128)(2,1)S(1)} %normalize.1.refs_0_, bf16[128,512]{1,0:T(8,128)(2,1)S(1)} %collective-permute-done.5.refs_1_), custom_call_target="tpu_custom_call" | custom-call | flops 1073741824 | bytes 4194304 | tf_op jit(solution)/shard_map/first_sums/pallas_call | solution.py:36
  22.0 0.3 %collective-permute-done.4.far_ref = bf16[64,512]{1,0:T(8,128)(2,1)S(1)} collective-permute-done((bf16[64,512]{1,0:T(8,128)(2,1)S(1)}, bf16[64,512]{1,0:T(8,128)(2,1)S(1)}, u32[]{:S(2)}, u32[]{:S(2)}) %collective-permute-start.4) | collective-permute-done | bytes 65568 | tf_op jit(solution)/shard_map/ppermute | solution.py:293
  22.4 1.6 %collective-permute-start.7 = (bf16[128,512]{1,0:T(8,128)(2,1)S(1)}, bf16[128,512]{1,0:T(8,128)(2,1)S(1)}, u32[]{:S(2)}, u32[]{:S(2)}) collective-permute-start(bf16[128,512]{1,0:T(8,128)(2,1)S(1)} %all_tests.1.refs_0_), channel_id=1, source_target_pairs={{0,16},{8,24},{16,0},{24,8},{1,17},{9,25},{17,1},{25,9},{2,18},{10... | collective-permute-start | bytes 393224 | tf_op jit(solution)/shard_map/ppermute | solution.py:293
  24.0 0.0 collective-permute-done.10.refs_1_
  24.0 0.0 collective-permute-done.9.refs_0_
  24.0 1.3 %last_sums.1 = (f32[2,1024]{1,0:T(2,128)S(1)}, f32[2,1024]{1,0:T(2,128)S(1)}) custom-call(bf16[4096,512]{1,0:T(8,128)(2,1)S(1)} %unit_gallery.1.unit_ref, bf16[128,512]{1,0:T(8,128)(2,1)S(1)} %collective-permute-done.9.refs_0_, bf16[128,512]{1,0:T(8,128)(2,1)S(1)} %collective-permute-done.10.refs_1_, f32[8,4096]{1,0:T(8,128)S(1)} %first_sums.2.refs_2_, ...), custom_call_target="tpu_custom_call" | custom-call | flops 1073741824 | bytes 4194304 | tf_op jit(solution)/shard_map/last_sums/pallas_call | solution.py:36
  25.3 0.9 %collective-permute-start.11 = (f32[2,1024]{1,0:T(2,128)S(1)}, f32[2,1024]{1,0:T(2,128)S(1)}, u32[]{:S(2)}, u32[]{:S(2)}) collective-permute-start(f32[2,1024]{1,0:T(2,128)S(1)} %get-tuple-element.20), channel_id=1, source_target_pairs={{0,16},{8,24},{16,0},{24,8},{1,17},{9,25},{17,1},{25,9},{2,18},{10... | collective-permute-start | bytes 24584 | tf_op jit(solution)/shard_map/ppermute | solution.py:293
  26.2 1.3 %collective-permute-done.7.refs_2_ = bf16[128,512]{1,0:T(8,128)(2,1)S(1)} collective-permute-done((bf16[128,512]{1,0:T(8,128)(2,1)S(1)}, bf16[128,512]{1,0:T(8,128)(2,1)S(1)}, u32[]{:S(2)}, u32[]{:S(2)}) %collective-permute-start.7) | collective-permute-done | bytes 131104 | tf_op jit(solution)/shard_map/ppermute | solution.py:293
  27.5 0.0 collective-permute-start.8
  27.5 1.5 %collective-permute-done.11.received_ref = f32[2,1024]{1,0:T(2,128)S(1)} collective-permute-done((f32[2,1024]{1,0:T(2,128)S(1)}, f32[2,1024]{1,0:T(2,128)S(1)}, u32[]{:S(2)}, u32[]{:S(2)}) %collective-permute-start.11) | collective-permute-done | bytes 8224 | tf_op jit(solution)/shard_map/ppermute | solution.py:293
  29.0 0.1 collective-permute-start.12
  29.1 0.0 collective-permute-done.6.refs_1_
  29.1 0.7 %raw_scores.1.raw_ref = f32[512,1024]{1,0:T(8,128)S(1)} custom-call(bf16[4096,512]{1,0:T(8,128)(2,1)S(1)} %unit_gallery.1.unit_ref, bf16[128,512]{1,0:T(8,128)(2,1)S(1)} %all_tests.1.refs_0_, bf16[128,512]{1,0:T(8,128)(2,1)S(1)} %collective-permute-done.6.refs_1_, bf16[128,512]{1,0:T(8,128)(2,1)S(1)} %collective-permute-done.7.refs_2_, ...), custom_call_target="tpu_custom_call" | custom-call | flops 536870912 | bytes 2097152 | tf_op jit(solution)/shard_map/raw_scores/pallas_call | solution.py:36
  29.9 0.4 %collective-permute-done.12.far_ref = f32[1,1024]{1,0:T(1,128)S(1)} collective-permute-done((f32[1,1024]{1,0:T(1,128)S(1)}, f32[1,1024]{1,0:T(1,128)S(1)}, u32[]{:S(2)}, u32[]{:S(2)}) %collective-permute-start.12) | collective-permute-done | bytes 4128 | tf_op jit(solution)/shard_map/ppermute | solution.py:293
  30.3 1.5 %write_scores.1 = f32[4096,128]{1,0:T(8,128)} custom-call(s32[1]{0:T(128)} %bitcast.bank_ref, f32[512,1024]{1,0:T(8,128)S(1)} %raw_scores.1.raw_ref, f32[2,1024]{1,0:T(2,128)S(1)} %get-tuple-element.19.keep_ref, f32[2,1024]{1,0:T(2,128)S(1)} %collective-permute-done.11.received_ref, f32[1,1024]{1,0:T(1,128)S(1)} %collective-permute-done.12.far_ref), custom_call_target="tpu_custom_call" | custom-call | flops 524288 | bytes 4194304 | tf_op jit(solution)/shard_map/write_scores/pallas_call | solution.py:36
  (5 shorter events, 0.0 us)
Async XLA Ops:
  0.0 11.2 %collective-permute-start.1 = (bf16[128,512]{1,0:T(8,128)(2,1)}, bf16[128,512]{1,0:T(8,128)(2,1)S(1)}, u32[]{:S(2)}, u32[]{:S(2)}) collective-permute-start(bf16[128,512]{1,0:T(8,128)(2,1)} %captions_ref.1), channel_id=1, source_target_pairs={{0,4},{1,5},{2,6},{3,7},{4,0},{5,1},{6,2},{7,3},{8,12},{9,13},{10,... | collective-permute-start | bytes 393224 | tf_op jit(solution)/shard_map/ppermute | solution.py:293
  5.1 9.3 %collective-permute-start.3 = (bf16[144,512]{1,0:T(8,128)(2,1)S(1)}, bf16[144,512]{1,0:T(8,128)(2,1)S(1)}, u32[]{:S(2)}, u32[]{:S(2)}) collective-permute-start(bf16[144,512]{1,0:T(8,128)(2,1)S(1)} %prepare.1.refs_0_), channel_id=1, source_target_pairs={{0,3},{1,2},{2,1},{3,0},{4,7},{5,6},{6,5},{7,4},{8,11},{9,10},{10,... | collective-permute-start | bytes 442376 | tf_op jit(solution)/shard_map/ppermute | solution.py:293
  7.7 9.3 %collective-permute-start.2 = (bf16[144,512]{1,0:T(8,128)(2,1)S(1)}, bf16[144,512]{1,0:T(8,128)(2,1)S(1)}, u32[]{:S(2)}, u32[]{:S(2)}) collective-permute-start(bf16[144,512]{1,0:T(8,128)(2,1)S(1)} %prepare.1.refs_0_), channel_id=1, source_target_pairs={{0,2},{1,3},{2,0},{3,1},{4,6},{5,7},{6,4},{7,5},{8,10},{9,11},{10,... | collective-permute-start | bytes 442376 | tf_op jit(solution)/shard_map/ppermute | solution.py:293
  8.1 8.8 %collective-permute-start = (bf16[144,512]{1,0:T(8,128)(2,1)S(1)}, bf16[144,512]{1,0:T(8,128)(2,1)S(1)}, u32[]{:S(2)}, u32[]{:S(2)}) collective-permute-start(bf16[144,512]{1,0:T(8,128)(2,1)S(1)} %prepare.1.refs_0_), channel_id=1, source_target_pairs={{0,1},{1,0},{2,3},{3,2},{4,5},{5,4},{6,7},{7,6},{8,9},{9,8},{10,11... | collective-permute-start | bytes 442376 | tf_op jit(solution)/shard_map/ppermute | solution.py:293
  11.4 12.6 %collective-permute-start.10 = (bf16[128,512]{1,0:T(8,128)(2,1)S(1)}, bf16[128,512]{1,0:T(8,128)(2,1)S(1)}, u32[]{:S(2)}, u32[]{:S(2)}) collective-permute-start(bf16[128,512]{1,0:T(8,128)(2,1)S(1)} %normalize.1.refs_0_), channel_id=1, source_target_pairs={{0,3},{1,2},{2,1},{3,0},{4,7},{5,6},{6,5},{7,4},{8,11},{9,10},{10,... | collective-permute-start | bytes 393224 | tf_op jit(solution)/shard_map/ppermute | solution.py:293
  13.9 10.0 %collective-permute-start.9 = (bf16[128,512]{1,0:T(8,128)(2,1)S(1)}, bf16[128,512]{1,0:T(8,128)(2,1)S(1)}, u32[]{:S(2)}, u32[]{:S(2)}) collective-permute-start(bf16[128,512]{1,0:T(8,128)(2,1)S(1)} %normalize.1.refs_0_), channel_id=1, source_target_pairs={{0,2},{1,3},{2,0},{3,1},{4,6},{5,7},{6,4},{7,5},{8,10},{9,11},{10,... | collective-permute-start | bytes 393224 | tf_op jit(solution)/shard_map/ppermute | solution.py:293
  14.4 6.3 %collective-permute-start.5 = (bf16[128,512]{1,0:T(8,128)(2,1)S(1)}, bf16[128,512]{1,0:T(8,128)(2,1)S(1)}, u32[]{:S(2)}, u32[]{:S(2)}) collective-permute-start(bf16[128,512]{1,0:T(8,128)(2,1)S(1)} %normalize.1.refs_0_), channel_id=1, source_target_pairs={{0,1},{1,0},{2,3},{3,2},{4,5},{5,4},{6,7},{7,6},{8,9},{9,8},{10,11... | collective-permute-start | bytes 393224 | tf_op jit(solution)/shard_map/ppermute | solution.py:293
  17.0 5.4 %collective-permute-start.4 = (bf16[64,512]{1,0:T(8,128)(2,1)S(1)}, bf16[64,512]{1,0:T(8,128)(2,1)S(1)}, u32[]{:S(2)}, u32[]{:S(2)}) collective-permute-start(bf16[64,512]{1,0:T(8,128)(2,1)S(1)} %near_tests.1.near_ref), channel_id=1, source_target_pairs={{0,4},{1,5},{2,6},{3,7},{4,0},{5,1},{6,2},{7,3},{8,12},{9,13},{10,... | collective-permute-start | bytes 196616 | tf_op jit(solution)/shard_map/ppermute | solution.py:293
  22.4 5.1 %collective-permute-start.7 = (bf16[128,512]{1,0:T(8,128)(2,1)S(1)}, bf16[128,512]{1,0:T(8,128)(2,1)S(1)}, u32[]{:S(2)}, u32[]{:S(2)}) collective-permute-start(bf16[128,512]{1,0:T(8,128)(2,1)S(1)} %all_tests.1.refs_0_), channel_id=1, source_target_pairs={{0,16},{8,24},{16,0},{24,8},{1,17},{9,25},{17,1},{25,9},{2,18},{10... | collective-permute-start | bytes 393224 | tf_op jit(solution)/shard_map/ppermute | solution.py:293
  25.3 3.7 %collective-permute-start.11 = (f32[2,1024]{1,0:T(2,128)S(1)}, f32[2,1024]{1,0:T(2,128)S(1)}, u32[]{:S(2)}, u32[]{:S(2)}) collective-permute-start(f32[2,1024]{1,0:T(2,128)S(1)} %get-tuple-element.20), channel_id=1, source_target_pairs={{0,16},{8,24},{16,0},{24,8},{1,17},{9,25},{17,1},{25,9},{2,18},{10... | collective-permute-start | bytes 24584 | tf_op jit(solution)/shard_map/ppermute | solution.py:293
  26.2 2.9 %collective-permute-start.6 = (bf16[128,512]{1,0:T(8,128)(2,1)S(1)}, bf16[128,512]{1,0:T(8,128)(2,1)S(1)}, u32[]{:S(2)}, u32[]{:S(2)}) collective-permute-start(bf16[128,512]{1,0:T(8,128)(2,1)S(1)} %all_tests.1.refs_0_), channel_id=1, source_target_pairs={{0,8},{8,0},{16,24},{24,16},{1,9},{9,1},{17,25},{25,17},{2,10},{10... | collective-permute-start | bytes 393224 | tf_op jit(solution)/shard_map/ppermute | solution.py:293
  27.5 1.6 %collective-permute-start.8 = (bf16[128,512]{1,0:T(8,128)(2,1)S(1)}, bf16[128,512]{1,0:T(8,128)(2,1)S(1)}, u32[]{:S(2)}, u32[]{:S(2)}) collective-permute-start(bf16[128,512]{1,0:T(8,128)(2,1)S(1)} %collective-permute-done.7.refs_2_), channel_id=1, source_target_pairs={{0,8},{8,0},{16,24},{24,16},{1,9},{9,1},{17,25},{25,17},{2,10},{10... | collective-permute-start | bytes 393224 | tf_op jit(solution)/shard_map/ppermute | solution.py:293
  29.0 1.2 %collective-permute-start.12 = (f32[1,1024]{1,0:T(1,128)S(1)}, f32[1,1024]{1,0:T(1,128)S(1)}, u32[]{:S(2)}, u32[]{:S(2)}) collective-permute-start(f32[1,1024]{1,0:T(1,128)S(1)} %slice_add_fusion), channel_id=1, source_target_pairs={{0,8},{8,0},{16,24},{24,16},{1,9},{9,1},{17,25},{25,17},{2,10},{10... | collective-permute-start | bytes 12296 | tf_op jit(solution)/shard_map/ppermute | solution.py:293

commit v5 on v4

--- a/solution.py
+++ b/solution.py
@@ -30,6 +30,13 @@
 def exp_sums(captions, clips):
     grown = jnp.exp2(products(captions, clips) * (inverse_temp * log2_e))
     return jnp.sum(grown.reshape(grown.shape[0] // 8, 8, grown.shape[1]), axis=0)
+
+
+def all_sums(captions, clips):
+    parts = [
+        exp_sums(jnp.concatenate(captions[k : k + 4], axis=0), clips) for k in range(0, len(captions), 4)
+    ]
+    return sum(parts[1:], parts[0])
 
 
 def call(kernel, name, out_shape, flops, moved, *args, in_specs, out_specs=in_vmem, scratch=()):
@@ -136,11 +143,9 @@
     count = len(payloads)
 
     def kernel(unit_ref, *refs):
-        captions = jnp.concatenate(
-            [ref[:rows, :] for ref in refs[:done]] + [unit_rows(ref[...]) for ref in refs[done:count]],
-            axis=0,
-        )
-        refs[count][...] = exp_sums(captions, unit_ref[...])
+        captions = [ref[:rows, :] for ref in refs[:done]]
+        captions += [unit_rows(ref[...]) for ref in refs[done:count]]
+        refs[count][...] = all_sums(captions, unit_ref[...])
 
     return call(
         kernel,
@@ -160,8 +165,7 @@
     half = clips // share // 2
 
     def kernel(unit_ref, *refs):
-        captions = jnp.concatenate([ref[...] for ref in refs[:count]], axis=0)
-        total = exp_sums(captions, unit_ref[...])
+        total = all_sums([ref[...] for ref in refs[:count]], unit_ref[...])
         for ref in refs[count : count + parts]:
             total = total + ref[...]
         total = jnp.sum(total, axis=0, keepdims=True)
@@ -322,7 +326,7 @@
     tests_both = swap(tests_y, "bank", 1)
     raw = raw_scores(unit, [tests, tests_core, tests_y, tests_both], share)
 
-    keep, send = last_sums(unit, [after(last[1], tests), after(last[2], tests)], sums, rows, share)
+    keep, send = last_sums(unit, [after(came, tests) for came in last[1:]], sums, rows, share)
     received = swap(send, "bank", 2)
     other = swap(keep[1:] + received[1:], "bank", 1)
     result = write_scores(bank, raw, keep, received, other, groups, rows * shards * groups)

time: 32 us -> 32 us (level)
  no operation moved by 1% of the time
where the time goes in v5:
time: 32 us; the launch traced here: 31.7 us
  starting transfers between devices  14.6 us (46%)
  Pallas kernels  11 us (34%)
  waiting for transfers between devices  6.05 us (19%)
    ppermute x13, starting transfers between devices, swap(): return lax.ppermute(values, axis, [(i, i ^ mask) for i in range(size)])  14.6 us
    pallas_call x10, Pallas kernels, call(): pl.pallas_call(kernel, out_shape=out_shape, in_specs=in_specs, out_specs=...  11 us
    ppermute x13, waiting for transfers between devices, swap(): return lax.ppermute(values, axis, [(i, i ^ mask) for i in range(size)])  6.05 us
  transfers between devices with their start and end apart: 13, of which 6 were waited for; matrix products, arithmetic and copies ran while one was open for 0% of the time, Pallas kernels for 30%

profile of v5, /device:TPU:0, one launch (start us, length us, event | category | flops | bytes accessed | tf_op | source)
XLA Modules:
  0.0 31.7 jit_solution(292784041734885407)
XLA Ops:
  0.0 4.0 %collective-permute-start.1 = (bf16[128,512]{1,0:T(8,128)(2,1)}, bf16[128,512]{1,0:T(8,128)(2,1)S(1)}, u32[]{:S(2)}, u32[]{:S(2)}) collective-permute-start(bf16[128,512]{1,0:T(8,128)(2,1)} %captions_ref.1), channel_id=1, source_target_pairs={{0,4},{1,5},{2,6},{3,7},{4,0},{5,1},{6,2},{7,3},{8,12},{9,13},{10,... | collective-permute-start | bytes 393224 | tf_op jit(solution)/shard_map/ppermute | solution.py:297
  4.0 1.1 %prepare.1.refs_0_ = bf16[144,512]{1,0:T(8,128)(2,1)S(1)} custom-call(bf16[128,512]{1,0:T(8,128)(2,1)} %captions_ref.1, bf16[16,512]{1,0:T(8,128)(2,1)} %tests_ref.1), custom_call_target="tpu_custom_call" | custom-call | flops 65536 | bytes 262144 | tf_op jit(solution)/shard_map/prepare/pallas_call | solution.py:43
  5.1 2.6 %collective-permute-start.3 = (bf16[144,512]{1,0:T(8,128)(2,1)S(1)}, bf16[144,512]{1,0:T(8,128)(2,1)S(1)}, u32[]{:S(2)}, u32[]{:S(2)}) collective-permute-start(bf16[144,512]{1,0:T(8,128)(2,1)S(1)} %prepare.1.refs_0_), channel_id=1, source_target_pairs={{0,3},{1,2},{2,1},{3,0},{4,7},{5,6},{6,5},{7,4},{8,11},{9,10},{10,... | collective-permute-start | bytes 442376 | tf_op jit(solution)/shard_map/ppermute | solution.py:297
  7.7 0.4 %collective-permute-start.2 = (bf16[144,512]{1,0:T(8,128)(2,1)S(1)}, bf16[144,512]{1,0:T(8,128)(2,1)S(1)}, u32[]{:S(2)}, u32[]{:S(2)}) collective-permute-start(bf16[144,512]{1,0:T(8,128)(2,1)S(1)} %prepare.1.refs_0_), channel_id=1, source_target_pairs={{0,2},{1,3},{2,0},{3,1},{4,6},{5,7},{6,4},{7,5},{8,10},{9,11},{10,... | collective-permute-start | bytes 442376 | tf_op jit(solution)/shard_map/ppermute | solution.py:297
  8.1 0.5 %collective-permute-start = (bf16[144,512]{1,0:T(8,128)(2,1)S(1)}, bf16[144,512]{1,0:T(8,128)(2,1)S(1)}, u32[]{:S(2)}, u32[]{:S(2)}) collective-permute-start(bf16[144,512]{1,0:T(8,128)(2,1)S(1)} %prepare.1.refs_0_), channel_id=1, source_target_pairs={{0,1},{1,0},{2,3},{3,2},{4,5},{5,4},{6,7},{7,6},{8,9},{9,8},{10,11... | collective-permute-start | bytes 442376 | tf_op jit(solution)/shard_map/ppermute | solution.py:297
  8.7 2.6 %unit_gallery.1.unit_ref = bf16[4096,512]{1,0:T(8,128)(2,1)S(1)} custom-call(s32[1]{0:T(128)} %bitcast.bank_ref, bf16[4096,512]{1,0:T(8,128)(2,1)} %gallery_ref.1), custom_call_target="tpu_custom_call" | custom-call | flops 8388608 | bytes 8388608 | tf_op jit(solution)/shard_map/unit_gallery/pallas_call | solution.py:43
  11.2 0.0 collective-permute-done.1.captions_ref
  11.3 0.1 normalize.1.refs_0_
  11.4 2.6 %collective-permute-start.10 = (bf16[128,512]{1,0:T(8,128)(2,1)S(1)}, bf16[128,512]{1,0:T(8,128)(2,1)S(1)}, u32[]{:S(2)}, u32[]{:S(2)}) collective-permute-start(bf16[128,512]{1,0:T(8,128)(2,1)S(1)} %normalize.1.refs_0_), channel_id=1, source_target_pairs={{0,3},{1,2},{2,1},{3,0},{4,7},{5,6},{6,5},{7,4},{8,11},{9,10},{10,... | collective-permute-start | bytes 393224 | tf_op jit(solution)/shard_map/ppermute | solution.py:297
  13.9 0.4 %collective-permute-start.9 = (bf16[128,512]{1,0:T(8,128)(2,1)S(1)}, bf16[128,512]{1,0:T(8,128)(2,1)S(1)}, u32[]{:S(2)}, u32[]{:S(2)}) collective-permute-start(bf16[128,512]{1,0:T(8,128)(2,1)S(1)} %normalize.1.refs_0_), channel_id=1, source_target_pairs={{0,2},{1,3},{2,0},{3,1},{4,6},{5,7},{6,4},{7,5},{8,10},{9,11},{10,... | collective-permute-start | bytes 393224 | tf_op jit(solution)/shard_map/ppermute | solution.py:297
  14.4 0.0 collective-permute-done.3.refs_3_
  14.4 0.9 %collective-permute-start.5 = (bf16[128,512]{1,0:T(8,128)(2,1)S(1)}, bf16[128,512]{1,0:T(8,128)(2,1)S(1)}, u32[]{:S(2)}, u32[]{:S(2)}) collective-permute-start(bf16[128,512]{1,0:T(8,128)(2,1)S(1)} %normalize.1.refs_0_), channel_id=1, source_target_pairs={{0,1},{1,0},{2,3},{3,2},{4,5},{5,4},{6,7},{7,6},{8,9},{9,8},{10,11... | collective-permute-start | bytes 393224 | tf_op jit(solution)/shard_map/ppermute | solution.py:297
  15.3 1.7 %collective-permute-done.2.refs_2_ = bf16[144,512]{1,0:T(8,128)(2,1)S(1)} collective-permute-done((bf16[144,512]{1,0:T(8,128)(2,1)S(1)}, bf16[144,512]{1,0:T(8,128)(2,1)S(1)}, u32[]{:S(2)}, u32[]{:S(2)}) %collective-permute-start.2) | collective-permute-done | bytes 147488 | tf_op jit(solution)/shard_map/ppermute | solution.py:297
  16.9 0.0 collective-permute-done.refs_1_
  17.0 0.5 %collective-permute-start.4 = (bf16[64,512]{1,0:T(8,128)(2,1)S(1)}, bf16[64,512]{1,0:T(8,128)(2,1)S(1)}, u32[]{:S(2)}, u32[]{:S(2)}) collective-permute-start(bf16[64,512]{1,0:T(8,128)(2,1)S(1)} %near_tests.1.near_ref), channel_id=1, source_target_pairs={{0,4},{1,5},{2,6},{3,7},{4,0},{5,1},{6,2},{7,3},{8,12},{9,13},{10,... | collective-permute-start | bytes 196616 | tf_op jit(solution)/shard_map/ppermute | solution.py:297
  17.5 2.4 %first_sums.2.refs_2_ = f32[8,4096]{1,0:T(8,128)S(1)} custom-call(bf16[4096,512]{1,0:T(8,128)(2,1)S(1)} %unit_gallery.1.unit_ref, bf16[144,512]{1,0:T(8,128)(2,1)S(1)} %prepare.1.refs_0_, bf16[144,512]{1,0:T(8,128)(2,1)S(1)} %collective-permute-done.refs_1_, bf16[144,512]{1,0:T(8,128)(2,1)S(1)} %collective-permute-done.2.refs_2_, ...), custom_call_target="tpu_custom_call" | custom-call | flops 2147483648 | bytes 4194304 | tf_op jit(solution)/shard_map/first_sums/pallas_call | solution.py:43
  19.9 0.8 %collective-permute-done.5.refs_1_ = bf16[128,512]{1,0:T(8,128)(2,1)S(1)} collective-permute-done((bf16[128,512]{1,0:T(8,128)(2,1)S(1)}, bf16[128,512]{1,0:T(8,128)(2,1)S(1)}, u32[]{:S(2)}, u32[]{:S(2)}) %collective-permute-start.5) | collective-permute-done | bytes 131104 | tf_op jit(solution)/shard_map/ppermute | solution.py:297
  20.7 1.3 %first_sums.3.refs_3_ = f32[8,4096]{1,0:T(8,128)S(1)} custom-call(bf16[4096,512]{1,0:T(8,128)(2,1)S(1)} %unit_gallery.1.unit_ref, bf16[128,512]{1,0:T(8,128)(2,1)S(1)} %normalize.1.refs_0_, bf16[128,512]{1,0:T(8,128)(2,1)S(1)} %collective-permute-done.5.refs_1_), custom_call_target="tpu_custom_call" | custom-call | flops 1073741824 | bytes 4194304 | tf_op jit(solution)/shard_map/first_sums/pallas_call | solution.py:43
  22.0 0.3 %collective-permute-done.4.far_ref = bf16[64,512]{1,0:T(8,128)(2,1)S(1)} collective-permute-done((bf16[64,512]{1,0:T(8,128)(2,1)S(1)}, bf16[64,512]{1,0:T(8,128)(2,1)S(1)}, u32[]{:S(2)}, u32[]{:S(2)}) %collective-permute-start.4) | collective-permute-done | bytes 65568 | tf_op jit(solution)/shard_map/ppermute | solution.py:297
  22.4 1.6 %collective-permute-start.7 = (bf16[128,512]{1,0:T(8,128)(2,1)S(1)}, bf16[128,512]{1,0:T(8,128)(2,1)S(1)}, u32[]{:S(2)}, u32[]{:S(2)}) collective-permute-start(bf16[128,512]{1,0:T(8,128)(2,1)S(1)} %all_tests.1.refs_0_), channel_id=1, source_target_pairs={{0,16},{8,24},{16,0},{24,8},{1,17},{9,25},{17,1},{25,9},{2,18},{10... | collective-permute-start | bytes 393224 | tf_op jit(solution)/shard_map/ppermute | solution.py:297
  24.0 0.0 collective-permute-done.10.refs_1_
  24.0 0.0 collective-permute-done.9.refs_0_
  24.0 1.3 %last_sums.1 = (f32[2,1024]{1,0:T(2,128)S(1)}, f32[2,1024]{1,0:T(2,128)S(1)}) custom-call(bf16[4096,512]{1,0:T(8,128)(2,1)S(1)} %unit_gallery.1.unit_ref, bf16[128,512]{1,0:T(8,128)(2,1)S(1)} %collective-permute-done.9.refs_0_, bf16[128,512]{1,0:T(8,128)(2,1)S(1)} %collective-permute-done.10.refs_1_, f32[8,4096]{1,0:T(8,128)S(1)} %first_sums.2.refs_2_, ...), custom_call_target="tpu_custom_call" | custom-call | flops 1073741824 | bytes 4194304 | tf_op jit(solution)/shard_map/last_sums/pallas_call | solution.py:43
  25.3 0.9 %collective-permute-start.11 = (f32[2,1024]{1,0:T(2,128)S(1)}, f32[2,1024]{1,0:T(2,128)S(1)}, u32[]{:S(2)}, u32[]{:S(2)}) collective-permute-start(f32[2,1024]{1,0:T(2,128)S(1)} %get-tuple-element.20), channel_id=1, source_target_pairs={{0,16},{8,24},{16,0},{24,8},{1,17},{9,25},{17,1},{25,9},{2,18},{10... | collective-permute-start | bytes 24584 | tf_op jit(solution)/shard_map/ppermute | solution.py:297
  26.2 1.3 %collective-permute-done.7.refs_2_ = bf16[128,512]{1,0:T(8,128)(2,1)S(1)} collective-permute-done((bf16[128,512]{1,0:T(8,128)(2,1)S(1)}, bf16[128,512]{1,0:T(8,128)(2,1)S(1)}, u32[]{:S(2)}, u32[]{:S(2)}) %collective-permute-start.7) | collective-permute-done | bytes 131104 | tf_op jit(solution)/shard_map/ppermute | solution.py:297
  27.5 0.0 collective-permute-start.8
  27.5 1.5 %collective-permute-done.11.received_ref = f32[2,1024]{1,0:T(2,128)S(1)} collective-permute-done((f32[2,1024]{1,0:T(2,128)S(1)}, f32[2,1024]{1,0:T(2,128)S(1)}, u32[]{:S(2)}, u32[]{:S(2)}) %collective-permute-start.11) | collective-permute-done | bytes 8224 | tf_op jit(solution)/shard_map/ppermute | solution.py:297
  29.0 0.1 collective-permute-start.12
  29.1 0.0 collective-permute-done.6.refs_1_
  29.1 0.7 %raw_scores.1.raw_ref = f32[512,1024]{1,0:T(8,128)S(1)} custom-call(bf16[4096,512]{1,0:T(8,128)(2,1)S(1)} %unit_gallery.1.unit_ref, bf16[128,512]{1,0:T(8,128)(2,1)S(1)} %all_tests.1.refs_0_, bf16[128,512]{1,0:T(8,128)(2,1)S(1)} %collective-permute-done.6.refs_1_, bf16[128,512]{1,0:T(8,128)(2,1)S(1)} %collective-permute-done.7.refs_2_, ...), custom_call_target="tpu_custom_call" | custom-call | flops 536870912 | bytes 2097152 | tf_op jit(solution)/shard_map/raw_scores/pallas_call | solution.py:43
  29.9 0.4 %collective-permute-done.12.far_ref = f32[1,1024]{1,0:T(1,128)S(1)} collective-permute-done((f32[1,1024]{1,0:T(1,128)S(1)}, f32[1,1024]{1,0:T(1,128)S(1)}, u32[]{:S(2)}, u32[]{:S(2)}) %collective-permute-start.12) | collective-permute-done | bytes 4128 | tf_op jit(solution)/shard_map/ppermute | solution.py:297
  30.3 1.5 %write_scores.1 = f32[4096,128]{1,0:T(8,128)} custom-call(s32[1]{0:T(128)} %bitcast.bank_ref, f32[512,1024]{1,0:T(8,128)S(1)} %raw_scores.1.raw_ref, f32[2,1024]{1,0:T(2,128)S(1)} %get-tuple-element.19.keep_ref, f32[2,1024]{1,0:T(2,128)S(1)} %collective-permute-done.11.received_ref, f32[1,1024]{1,0:T(1,128)S(1)} %collective-permute-done.12.far_ref), custom_call_target="tpu_custom_call" | custom-call | flops 524288 | bytes 4194304 | tf_op jit(solution)/shard_map/write_scores/pallas_call | solution.py:43
  (5 shorter events, 0.0 us)
Async XLA Ops:
  0.0 11.2 %collective-permute-start.1 = (bf16[128,512]{1,0:T(8,128)(2,1)}, bf16[128,512]{1,0:T(8,128)(2,1)S(1)}, u32[]{:S(2)}, u32[]{:S(2)}) collective-permute-start(bf16[128,512]{1,0:T(8,128)(2,1)} %captions_ref.1), channel_id=1, source_target_pairs={{0,4},{1,5},{2,6},{3,7},{4,0},{5,1},{6,2},{7,3},{8,12},{9,13},{10,... | collective-permute-start | bytes 393224 | tf_op jit(solution)/shard_map/ppermute | solution.py:297
  5.1 9.3 %collective-permute-start.3 = (bf16[144,512]{1,0:T(8,128)(2,1)S(1)}, bf16[144,512]{1,0:T(8,128)(2,1)S(1)}, u32[]{:S(2)}, u32[]{:S(2)}) collective-permute-start(bf16[144,512]{1,0:T(8,128)(2,1)S(1)} %prepare.1.refs_0_), channel_id=1, source_target_pairs={{0,3},{1,2},{2,1},{3,0},{4,7},{5,6},{6,5},{7,4},{8,11},{9,10},{10,... | collective-permute-start | bytes 442376 | tf_op jit(solution)/shard_map/ppermute | solution.py:297
  7.7 9.3 %collective-permute-start.2 = (bf16[144,512]{1,0:T(8,128)(2,1)S(1)}, bf16[144,512]{1,0:T(8,128)(2,1)S(1)}, u32[]{:S(2)}, u32[]{:S(2)}) collective-permute-start(bf16[144,512]{1,0:T(8,128)(2,1)S(1)} %prepare.1.refs_0_), channel_id=1, source_target_pairs={{0,2},{1,3},{2,0},{3,1},{4,6},{5,7},{6,4},{7,5},{8,10},{9,11},{10,... | collective-permute-start | bytes 442376 | tf_op jit(solution)/shard_map/ppermute | solution.py:297
  8.1 8.8 %collective-permute-start = (bf16[144,512]{1,0:T(8,128)(2,1)S(1)}, bf16[144,512]{1,0:T(8,128)(2,1)S(1)}, u32[]{:S(2)}, u32[]{:S(2)}) collective-permute-start(bf16[144,512]{1,0:T(8,128)(2,1)S(1)} %prepare.1.refs_0_), channel_id=1, source_target_pairs={{0,1},{1,0},{2,3},{3,2},{4,5},{5,4},{6,7},{7,6},{8,9},{9,8},{10,11... | collective-permute-start | bytes 442376 | tf_op jit(solution)/shard_map/ppermute | solution.py:297
  11.4 12.6 %collective-permute-start.10 = (bf16[128,512]{1,0:T(8,128)(2,1)S(1)}, bf16[128,512]{1,0:T(8,128)(2,1)S(1)}, u32[]{:S(2)}, u32[]{:S(2)}) collective-permute-start(bf16[128,512]{1,0:T(8,128)(2,1)S(1)} %normalize.1.refs_0_), channel_id=1, source_target_pairs={{0,3},{1,2},{2,1},{3,0},{4,7},{5,6},{6,5},{7,4},{8,11},{9,10},{10,... | collective-permute-start | bytes 393224 | tf_op jit(solution)/shard_map/ppermute | solution.py:297
  13.9 10.0 %collective-permute-start.9 = (bf16[128,512]{1,0:T(8,128)(2,1)S(1)}, bf16[128,512]{1,0:T(8,128)(2,1)S(1)}, u32[]{:S(2)}, u32[]{:S(2)}) collective-permute-start(bf16[128,512]{1,0:T(8,128)(2,1)S(1)} %normalize.1.refs_0_), channel_id=1, source_target_pairs={{0,2},{1,3},{2,0},{3,1},{4,6},{5,7},{6,4},{7,5},{8,10},{9,11},{10,... | collective-permute-start | bytes 393224 | tf_op jit(solution)/shard_map/ppermute | solution.py:297
  14.4 6.3 %collective-permute-start.5 = (bf16[128,512]{1,0:T(8,128)(2,1)S(1)}, bf16[128,512]{1,0:T(8,128)(2,1)S(1)}, u32[]{:S(2)}, u32[]{:S(2)}) collective-permute-start(bf16[128,512]{1,0:T(8,128)(2,1)S(1)} %normalize.1.refs_0_), channel_id=1, source_target_pairs={{0,1},{1,0},{2,3},{3,2},{4,5},{5,4},{6,7},{7,6},{8,9},{9,8},{10,11... | collective-permute-start | bytes 393224 | tf_op jit(solution)/shard_map/ppermute | solution.py:297
  17.0 5.4 %collective-permute-start.4 = (bf16[64,512]{1,0:T(8,128)(2,1)S(1)}, bf16[64,512]{1,0:T(8,128)(2,1)S(1)}, u32[]{:S(2)}, u32[]{:S(2)}) collective-permute-start(bf16[64,512]{1,0:T(8,128)(2,1)S(1)} %near_tests.1.near_ref), channel_id=1, source_target_pairs={{0,4},{1,5},{2,6},{3,7},{4,0},{5,1},{6,2},{7,3},{8,12},{9,13},{10,... | collective-permute-start | bytes 196616 | tf_op jit(solution)/shard_map/ppermute | solution.py:297
  22.4 5.1 %collective-permute-start.7 = (bf16[128,512]{1,0:T(8,128)(2,1)S(1)}, bf16[128,512]{1,0:T(8,128)(2,1)S(1)}, u32[]{:S(2)}, u32[]{:S(2)}) collective-permute-start(bf16[128,512]{1,0:T(8,128)(2,1)S(1)} %all_tests.1.refs_0_), channel_id=1, source_target_pairs={{0,16},{8,24},{16,0},{24,8},{1,17},{9,25},{17,1},{25,9},{2,18},{10... | collective-permute-start | bytes 393224 | tf_op jit(solution)/shard_map/ppermute | solution.py:297
  25.3 3.7 %collective-permute-start.11 = (f32[2,1024]{1,0:T(2,128)S(1)}, f32[2,1024]{1,0:T(2,128)S(1)}, u32[]{:S(2)}, u32[]{:S(2)}) collective-permute-start(f32[2,1024]{1,0:T(2,128)S(1)} %get-tuple-element.20), channel_id=1, source_target_pairs={{0,16},{8,24},{16,0},{24,8},{1,17},{9,25},{17,1},{25,9},{2,18},{10... | collective-permute-start | bytes 24584 | tf_op jit(solution)/shard_map/ppermute | solution.py:297
  26.2 2.9 %collective-permute-start.6 = (bf16[128,512]{1,0:T(8,128)(2,1)S(1)}, bf16[128,512]{1,0:T(8,128)(2,1)S(1)}, u32[]{:S(2)}, u32[]{:S(2)}) collective-permute-start(bf16[128,512]{1,0:T(8,128)(2,1)S(1)} %all_tests.1.refs_0_), channel_id=1, source_target_pairs={{0,8},{8,0},{16,24},{24,16},{1,9},{9,1},{17,25},{25,17},{2,10},{10... | collective-permute-start | bytes 393224 | tf_op jit(solution)/shard_map/ppermute | solution.py:297
  27.5 1.6 %collective-permute-start.8 = (bf16[128,512]{1,0:T(8,128)(2,1)S(1)}, bf16[128,512]{1,0:T(8,128)(2,1)S(1)}, u32[]{:S(2)}, u32[]{:S(2)}) collective-permute-start(bf16[128,512]{1,0:T(8,128)(2,1)S(1)} %collective-permute-done.7.refs_2_), channel_id=1, source_target_pairs={{0,8},{8,0},{16,24},{24,16},{1,9},{9,1},{17,25},{25,17},{2,10},{10... | collective-permute-start | bytes 393224 | tf_op jit(solution)/shard_map/ppermute | solution.py:297
  29.0 1.2 %collective-permute-start.12 = (f32[1,1024]{1,0:T(1,128)S(1)}, f32[1,1024]{1,0:T(1,128)S(1)}, u32[]{:S(2)}, u32[]{:S(2)}) collective-permute-start(f32[1,1024]{1,0:T(1,128)S(1)} %slice_add_fusion), channel_id=1, source_target_pairs={{0,8},{8,0},{16,24},{24,16},{1,9},{9,1},{17,25},{25,17},{2,10},{10... | collective-permute-start | bytes 12296 | tf_op jit(solution)/shard_map/ppermute | solution.py:297

commit v6 on v5

--- a/solution.py
+++ b/solution.py
@@ -251,15 +251,17 @@
 
 
 def write_scores(bank, raw, keep, received, far, groups, total):
-    every, share = raw.shape
+    share = raw[0].shape[1]
+    every = raw[0].shape[0] + raw[1].shape[0]
     rows, per_row = every // groups, share // lanes
 
-    def kernel(bank_ref, raw_ref, keep_ref, received_ref, far_ref, out_ref, staged, sems):
+    def kernel(bank_ref, near_ref, away_ref, keep_ref, received_ref, far_ref, out_ref, staged, sems):
         normalizer = keep_ref[0:1, :] + received_ref[0:1, :] + far_ref[...]
         shift = jnp.log(normalizer / total)
         copies = []
         for mask in range(groups):
-            values = raw_ref[mask * rows : (mask + 1) * rows, :] - shift
+            raw_ref, at = (near_ref, mask) if mask < groups // 2 else (away_ref, mask - groups // 2)
+            values = raw_ref[at * rows : (at + 1) * rows, :] - shift
             for k in range(per_row):
                 staged[mask, pl.ds(k, rows, stride=per_row), :] = values[:, k * lanes : (k + 1) * lanes]
             begin = pl.multiple_of((bank_ref[0] ^ mask) * (rows * per_row), rows * per_row)
@@ -279,11 +281,11 @@
         every * share,
         8 * every * share,
         bank,
-        raw,
+        *raw,
         keep,
         received,
         far,
-        in_specs=[in_smem] + [in_vmem] * 4,
+        in_specs=[in_smem] + [in_vmem] * 5,
         out_specs=in_hbm,
         scratch=[
             pltpu.VMEM((groups, rows * per_row, lanes), jnp.float32),
@@ -321,10 +323,11 @@
 
     sums.append(first_sums(unit, [across, last[0]], [], rows))
     tests = all_tests(gal, here, after(there, sums), half)
-    tests_y = swap(tests, "bank", 2)
+    far = after(there, sums)
+    tests_y = all_tests(gal, swap(after(here, sums[0]), "bank", 2), swap(far, "bank", 2), half)
     tests_core = swap(tests, "bank", 1)
     tests_both = swap(tests_y, "bank", 1)
-    raw = raw_scores(unit, [tests, tests_core, tests_y, tests_both], share)
+    raw = [raw_scores(unit, [tests, tests_core], share), raw_scores(unit, [tests_y, tests_both], share)]
 
     keep, send = last_sums(unit, [after(came, tests) for came in last[1:]], sums, rows, share)
     received = swap(send, "bank", 2)

time: 32 us -> 31.9 us (level)
  waiting for transfers between devices: 6.05 us -> 4.46 us
  starting transfers between devices: 14.6 us -> 15.9 us
    ppermute x13 -> x14, waiting for transfers between devices: 6.05 us -> 4.46 us  [swap(): return lax.ppermute(values, axis, [(i, i ^ mask) for i in range(size)])]
    ppermute x13 -> x14, starting transfers between devices: 14.6 us -> 15.9 us  [swap(): return lax.ppermute(values, axis, [(i, i ^ mask) for i in range(size)])]
    pallas_call x10 -> x12, Pallas kernels: 11 us -> 11.2 us  [call(): pl.pallas_call(kernel, out_shape=out_shape, in_specs=in_specs, out_specs=...]
  transfers between devices with their start and end apart: 13 -> 14, of which waited for: 6 -> 4; matrix products, arithmetic and copies ran while one was open for 0% -> 0% of each run, Pallas kernels for 30% -> 31%
where the time goes in v6:
time: 31.9 us; the launch traced here: 31.7 us
  starting transfers between devices  15.9 us (50%)
  Pallas kernels  11.2 us (35%)
  waiting for transfers between devices  4.46 us (14%)
    ppermute x14, starting transfers between devices, swap(): return lax.ppermute(values, axis, [(i, i ^ mask) for i in range(size)])  15.9 us
    pallas_call x12, Pallas kernels, call(): pl.pallas_call(kernel, out_shape=out_shape, in_specs=in_specs, out_specs=...  11.2 us
    ppermute x14, waiting for transfers between devices, swap(): return lax.ppermute(values, axis, [(i, i ^ mask) for i in range(size)])  4.46 us
  transfers between devices with their start and end apart: 14, of which 4 were waited for; matrix products, arithmetic and copies ran while one was open for 0% of the time, Pallas kernels for 31%

profile of v6, /device:TPU:0, one launch (start us, length us, event | category | flops | bytes accessed | tf_op | source)
XLA Modules:
  0.0 31.7 jit_solution(3496769400384666410)
XLA Ops:
  0.0 4.0 %collective-permute-start.1 = (bf16[128,512]{1,0:T(8,128)(2,1)}, bf16[128,512]{1,0:T(8,128)(2,1)S(1)}, u32[]{:S(2)}, u32[]{:S(2)}) collective-permute-start(bf16[128,512]{1,0:T(8,128)(2,1)} %captions_ref.1), channel_id=1, source_target_pairs={{0,4},{1,5},{2,6},{3,7},{4,0},{5,1},{6,2},{7,3},{8,12},{9,13},{10,... | collective-permute-start | bytes 393224 | tf_op jit(solution)/shard_map/ppermute | solution.py:299
  4.0 1.1 %prepare.1.refs_0_ = bf16[144,512]{1,0:T(8,128)(2,1)S(1)} custom-call(bf16[128,512]{1,0:T(8,128)(2,1)} %captions_ref.1, bf16[16,512]{1,0:T(8,128)(2,1)} %tests_ref.1), custom_call_target="tpu_custom_call" | custom-call | flops 65536 | bytes 262144 | tf_op jit(solution)/shard_map/prepare/pallas_call | solution.py:43
  5.1 2.6 %collective-permute-start.3 = (bf16[144,512]{1,0:T(8,128)(2,1)S(1)}, bf16[144,512]{1,0:T(8,128)(2,1)S(1)}, u32[]{:S(2)}, u32[]{:S(2)}) collective-permute-start(bf16[144,512]{1,0:T(8,128)(2,1)S(1)} %prepare.1.refs_0_), channel_id=1, source_target_pairs={{0,3},{1,2},{2,1},{3,0},{4,7},{5,6},{6,5},{7,4},{8,11},{9,10},{10,... | collective-permute-start | bytes 442376 | tf_op jit(solution)/shard_map/ppermute | solution.py:299
  7.7 0.4 %collective-permute-start.2 = (bf16[144,512]{1,0:T(8,128)(2,1)S(1)}, bf16[144,512]{1,0:T(8,128)(2,1)S(1)}, u32[]{:S(2)}, u32[]{:S(2)}) collective-permute-start(bf16[144,512]{1,0:T(8,128)(2,1)S(1)} %prepare.1.refs_0_), channel_id=1, source_target_pairs={{0,2},{1,3},{2,0},{3,1},{4,6},{5,7},{6,4},{7,5},{8,10},{9,11},{10,... | collective-permute-start | bytes 442376 | tf_op jit(solution)/shard_map/ppermute | solution.py:299
  8.1 0.5 %collective-permute-start = (bf16[144,512]{1,0:T(8,128)(2,1)S(1)}, bf16[144,512]{1,0:T(8,128)(2,1)S(1)}, u32[]{:S(2)}, u32[]{:S(2)}) collective-permute-start(bf16[144,512]{1,0:T(8,128)(2,1)S(1)} %prepare.1.refs_0_), channel_id=1, source_target_pairs={{0,1},{1,0},{2,3},{3,2},{4,5},{5,4},{6,7},{7,6},{8,9},{9,8},{10,11... | collective-permute-start | bytes 442376 | tf_op jit(solution)/shard_map/ppermute | solution.py:299
  8.7 2.6 %unit_gallery.1.unit_ref = bf16[4096,512]{1,0:T(8,128)(2,1)S(1)} custom-call(s32[1]{0:T(128)} %bitcast.bank_ref, bf16[4096,512]{1,0:T(8,128)(2,1)} %gallery_ref.1), custom_call_target="tpu_custom_call" | custom-call | flops 8388608 | bytes 8388608 | tf_op jit(solution)/shard_map/unit_gallery/pallas_call | solution.py:43
  11.2 0.0 collective-permute-done.1.captions_ref
  11.3 0.1 normalize.1.refs_0_
  11.4 2.6 %collective-permute-start.11 = (bf16[128,512]{1,0:T(8,128)(2,1)S(1)}, bf16[128,512]{1,0:T(8,128)(2,1)S(1)}, u32[]{:S(2)}, u32[]{:S(2)}) collective-permute-start(bf16[128,512]{1,0:T(8,128)(2,1)S(1)} %normalize.1.refs_0_), channel_id=1, source_target_pairs={{0,3},{1,2},{2,1},{3,0},{4,7},{5,6},{6,5},{7,4},{8,11},{9,10},{10,... | collective-permute-start | bytes 393224 | tf_op jit(solution)/shard_map/ppermute | solution.py:299
  13.9 0.4 %collective-permute-start.10 = (bf16[128,512]{1,0:T(8,128)(2,1)S(1)}, bf16[128,512]{1,0:T(8,128)(2,1)S(1)}, u32[]{:S(2)}, u32[]{:S(2)}) collective-permute-start(bf16[128,512]{1,0:T(8,128)(2,1)S(1)} %normalize.1.refs_0_), channel_id=1, source_target_pairs={{0,2},{1,3},{2,0},{3,1},{4,6},{5,7},{6,4},{7,5},{8,10},{9,11},{10,... | collective-permute-start | bytes 393224 | tf_op jit(solution)/shard_map/ppermute | solution.py:299
  14.4 0.0 collective-permute-done.3.refs_3_
  14.4 0.9 %collective-permute-start.5 = (bf16[128,512]{1,0:T(8,128)(2,1)S(1)}, bf16[128,512]{1,0:T(8,128)(2,1)S(1)}, u32[]{:S(2)}, u32[]{:S(2)}) collective-permute-start(bf16[128,512]{1,0:T(8,128)(2,1)S(1)} %normalize.1.refs_0_), channel_id=1, source_target_pairs={{0,1},{1,0},{2,3},{3,2},{4,5},{5,4},{6,7},{7,6},{8,9},{9,8},{10,11... | collective-permute-start | bytes 393224 | tf_op jit(solution)/shard_map/ppermute | solution.py:299
  15.3 1.7 %collective-permute-done.2.refs_2_ = bf16[144,512]{1,0:T(8,128)(2,1)S(1)} collective-permute-done((bf16[144,512]{1,0:T(8,128)(2,1)S(1)}, bf16[144,512]{1,0:T(8,128)(2,1)S(1)}, u32[]{:S(2)}, u32[]{:S(2)}) %collective-permute-start.2) | collective-permute-done | bytes 147488 | tf_op jit(solution)/shard_map/ppermute | solution.py:299
  16.9 0.0 collective-permute-done.refs_1_
  17.0 0.5 %collective-permute-start.4 = (bf16[64,512]{1,0:T(8,128)(2,1)S(1)}, bf16[64,512]{1,0:T(8,128)(2,1)S(1)}, u32[]{:S(2)}, u32[]{:S(2)}) collective-permute-start(bf16[64,512]{1,0:T(8,128)(2,1)S(1)} %near_tests.1.near_ref), channel_id=1, source_target_pairs={{0,4},{1,5},{2,6},{3,7},{4,0},{5,1},{6,2},{7,3},{8,12},{9,13},{10,... | collective-permute-start | bytes 196616 | tf_op jit(solution)/shard_map/ppermute | solution.py:299
  17.5 2.4 %first_sums.2.refs_2_ = f32[8,4096]{1,0:T(8,128)S(1)} custom-call(bf16[4096,512]{1,0:T(8,128)(2,1)S(1)} %unit_gallery.1.unit_ref, bf16[144,512]{1,0:T(8,128)(2,1)S(1)} %prepare.1.refs_0_, bf16[144,512]{1,0:T(8,128)(2,1)S(1)} %collective-permute-done.refs_1_, bf16[144,512]{1,0:T(8,128)(2,1)S(1)} %collective-permute-done.2.refs_2_, ...), custom_call_target="tpu_custom_call" | custom-call | flops 2147483648 | bytes 4194304 | tf_op jit(solution)/shard_map/first_sums/pallas_call | solution.py:43
  19.9 1.6 %collective-permute-start.7 = (bf16[64,512]{1,0:T(8,128)(2,1)S(1)}, bf16[64,512]{1,0:T(8,128)(2,1)S(1)}, u32[]{:S(2)}, u32[]{:S(2)}) collective-permute-start(bf16[64,512]{1,0:T(8,128)(2,1)S(1)} %near_tests.1.near_ref), channel_id=1, source_target_pairs={{0,16},{8,24},{16,0},{24,8},{1,17},{9,25},{17,1},{25,9},{2,18},{10... | collective-permute-start | bytes 196616 | tf_op jit(solution)/shard_map/ppermute | solution.py:299
  21.5 0.0 collective-permute-done.5.refs_1_
  21.5 1.3 %first_sums.3.refs_3_ = f32[8,4096]{1,0:T(8,128)S(1)} custom-call(bf16[4096,512]{1,0:T(8,128)(2,1)S(1)} %unit_gallery.1.unit_ref, bf16[128,512]{1,0:T(8,128)(2,1)S(1)} %normalize.1.refs_0_, bf16[128,512]{1,0:T(8,128)(2,1)S(1)} %collective-permute-done.5.refs_1_), custom_call_target="tpu_custom_call" | custom-call | flops 1073741824 | bytes 4194304 | tf_op jit(solution)/shard_map/first_sums/pallas_call | solution.py:43
  22.8 0.0 collective-permute-done.4.far_ref
  22.8 1.1 %collective-permute-start.8 = (bf16[64,512]{1,0:T(8,128)(2,1)S(1)}, bf16[64,512]{1,0:T(8,128)(2,1)S(1)}, u32[]{:S(2)}, u32[]{:S(2)}) collective-permute-start(bf16[64,512]{1,0:T(8,128)(2,1)S(1)} %collective-permute-done.4.far_ref), channel_id=1, source_target_pairs={{0,16},{8,24},{16,0},{24,8},{1,17},{9,25},{17,1},{25,9},{2,18},{10... | collective-permute-start | bytes 196616 | tf_op jit(solution)/shard_map/ppermute | solution.py:299
  23.9 1.3 %last_sums.1 = (f32[2,1024]{1,0:T(2,128)S(1)}, f32[2,1024]{1,0:T(2,128)S(1)}) custom-call(bf16[4096,512]{1,0:T(8,128)(2,1)S(1)} %unit_gallery.1.unit_ref, bf16[128,512]{1,0:T(8,128)(2,1)S(1)} %collective-permute-done.10.refs_0_, bf16[128,512]{1,0:T(8,128)(2,1)S(1)} %collective-permute-done.11.refs_1_, f32[8,4096]{1,0:T(8,128)S(1)} %first_sums.2.refs_2_, ...), custom_call_target="tpu_custom_call" | custom-call | flops 1073741824 | bytes 4194304 | tf_op jit(solution)/shard_map/last_sums/pallas_call | solution.py:43
  25.2 1.1 %collective-permute-start.12 = (f32[2,1024]{1,0:T(2,128)S(1)}, f32[2,1024]{1,0:T(2,128)S(1)}, u32[]{:S(2)}, u32[]{:S(2)}) collective-permute-start(f32[2,1024]{1,0:T(2,128)S(1)} %get-tuple-element.22), channel_id=1, source_target_pairs={{0,16},{8,24},{16,0},{24,8},{1,17},{9,25},{17,1},{25,9},{2,18},{10... | collective-permute-start | bytes 24584 | tf_op jit(solution)/shard_map/ppermute | solution.py:299
  26.3 0.9 %collective-permute-done.8.far_ref = bf16[64,512]{1,0:T(8,128)(2,1)S(1)} collective-permute-done((bf16[64,512]{1,0:T(8,128)(2,1)S(1)}, bf16[64,512]{1,0:T(8,128)(2,1)S(1)}, u32[]{:S(2)}, u32[]{:S(2)}) %collective-permute-start.8) | collective-permute-done | bytes 65568 | tf_op jit(solution)/shard_map/ppermute | solution.py:299
  27.2 0.1 collective-permute-start.9
  27.3 1.7 %collective-permute-done.12.received_ref = f32[2,1024]{1,0:T(2,128)S(1)} collective-permute-done((f32[2,1024]{1,0:T(2,128)S(1)}, f32[2,1024]{1,0:T(2,128)S(1)}, u32[]{:S(2)}, u32[]{:S(2)}) %collective-permute-start.12) | collective-permute-done | bytes 8224 | tf_op jit(solution)/shard_map/ppermute | solution.py:299
  29.0 0.1 collective-permute-start.13
  29.0 0.0 collective-permute-done.6.refs_1_
  29.1 0.5 %raw_scores.2.near_ref = f32[256,1024]{1,0:T(8,128)S(1)} custom-call(bf16[4096,512]{1,0:T(8,128)(2,1)S(1)} %unit_gallery.1.unit_ref, bf16[128,512]{1,0:T(8,128)(2,1)S(1)} %all_tests.2.refs_0_, bf16[128,512]{1,0:T(8,128)(2,1)S(1)} %collective-permute-done.6.refs_1_), custom_call_target="tpu_custom_call" | custom-call | flops 268435456 | bytes 1048576 | tf_op jit(solution)/shard_map/raw_scores/pallas_call | solution.py:43
  29.5 0.5 %raw_scores.3.away_ref = f32[256,1024]{1,0:T(8,128)S(1)} custom-call(bf16[4096,512]{1,0:T(8,128)(2,1)S(1)} %unit_gallery.1.unit_ref, bf16[128,512]{1,0:T(8,128)(2,1)S(1)} %all_tests.3.refs_0_, bf16[128,512]{1,0:T(8,128)(2,1)S(1)} %collective-permute-done.9.refs_1_), custom_call_target="tpu_custom_call" | custom-call | flops 268435456 | bytes 1048576 | tf_op jit(solution)/shard_map/raw_scores/pallas_call | solution.py:43
  30.0 0.2 collective-permute-done.13.far_ref
  30.2 1.5 %write_scores.1 = f32[4096,128]{1,0:T(8,128)} custom-call(s32[1]{0:T(128)} %bitcast.bank_ref, f32[256,1024]{1,0:T(8,128)S(1)} %raw_scores.2.near_ref, f32[256,1024]{1,0:T(8,128)S(1)} %raw_scores.3.away_ref, f32[2,1024]{1,0:T(2,128)S(1)} %get-tuple-element.21.keep_ref, f32[2,1024]{1,0:T(2,128)S(1)} %collective-permute-done.12.received_ref, ...), custom_call_target="tpu_custom_call" | custom-call | flops 524288 | bytes 4194304 | tf_op jit(solution)/shard_map/write_scores/pallas_call | solution.py:43
  (9 shorter events, 0.1 us)
Async XLA Ops:
  0.0 11.2 %collective-permute-start.1 = (bf16[128,512]{1,0:T(8,128)(2,1)}, bf16[128,512]{1,0:T(8,128)(2,1)S(1)}, u32[]{:S(2)}, u32[]{:S(2)}) collective-permute-start(bf16[128,512]{1,0:T(8,128)(2,1)} %captions_ref.1), channel_id=1, source_target_pairs={{0,4},{1,5},{2,6},{3,7},{4,0},{5,1},{6,2},{7,3},{8,12},{9,13},{10,... | collective-permute-start | bytes 393224 | tf_op jit(solution)/shard_map/ppermute | solution.py:299
  5.1 9.3 %collective-permute-start.3 = (bf16[144,512]{1,0:T(8,128)(2,1)S(1)}, bf16[144,512]{1,0:T(8,128)(2,1)S(1)}, u32[]{:S(2)}, u32[]{:S(2)}) collective-permute-start(bf16[144,512]{1,0:T(8,128)(2,1)S(1)} %prepare.1.refs_0_), channel_id=1, source_target_pairs={{0,3},{1,2},{2,1},{3,0},{4,7},{5,6},{6,5},{7,4},{8,11},{9,10},{10,... | collective-permute-start | bytes 442376 | tf_op jit(solution)/shard_map/ppermute | solution.py:299
  7.7 9.3 %collective-permute-start.2 = (bf16[144,512]{1,0:T(8,128)(2,1)S(1)}, bf16[144,512]{1,0:T(8,128)(2,1)S(1)}, u32[]{:S(2)}, u32[]{:S(2)}) collective-permute-start(bf16[144,512]{1,0:T(8,128)(2,1)S(1)} %prepare.1.refs_0_), channel_id=1, source_target_pairs={{0,2},{1,3},{2,0},{3,1},{4,6},{5,7},{6,4},{7,5},{8,10},{9,11},{10,... | collective-permute-start | bytes 442376 | tf_op jit(solution)/shard_map/ppermute | solution.py:299
  8.1 8.8 %collective-permute-start = (bf16[144,512]{1,0:T(8,128)(2,1)S(1)}, bf16[144,512]{1,0:T(8,128)(2,1)S(1)}, u32[]{:S(2)}, u32[]{:S(2)}) collective-permute-start(bf16[144,512]{1,0:T(8,128)(2,1)S(1)} %prepare.1.refs_0_), channel_id=1, source_target_pairs={{0,1},{1,0},{2,3},{3,2},{4,5},{5,4},{6,7},{7,6},{8,9},{9,8},{10,11... | collective-permute-start | bytes 442376 | tf_op jit(solution)/shard_map/ppermute | solution.py:299
  11.4 12.5 %collective-permute-start.11 = (bf16[128,512]{1,0:T(8,128)(2,1)S(1)}, bf16[128,512]{1,0:T(8,128)(2,1)S(1)}, u32[]{:S(2)}, u32[]{:S(2)}) collective-permute-start(bf16[128,512]{1,0:T(8,128)(2,1)S(1)} %normalize.1.refs_0_), channel_id=1, source_target_pairs={{0,3},{1,2},{2,1},{3,0},{4,7},{5,6},{6,5},{7,4},{8,11},{9,10},{10,... | collective-permute-start | bytes 393224 | tf_op jit(solution)/shard_map/ppermute | solution.py:299
  13.9 10.0 %collective-permute-start.10 = (bf16[128,512]{1,0:T(8,128)(2,1)S(1)}, bf16[128,512]{1,0:T(8,128)(2,1)S(1)}, u32[]{:S(2)}, u32[]{:S(2)}) collective-permute-start(bf16[128,512]{1,0:T(8,128)(2,1)S(1)} %normalize.1.refs_0_), channel_id=1, source_target_pairs={{0,2},{1,3},{2,0},{3,1},{4,6},{5,7},{6,4},{7,5},{8,10},{9,11},{10,... | collective-permute-start | bytes 393224 | tf_op jit(solution)/shard_map/ppermute | solution.py:299
  14.4 7.1 %collective-permute-start.5 = (bf16[128,512]{1,0:T(8,128)(2,1)S(1)}, bf16[128,512]{1,0:T(8,128)(2,1)S(1)}, u32[]{:S(2)}, u32[]{:S(2)}) collective-permute-start(bf16[128,512]{1,0:T(8,128)(2,1)S(1)} %normalize.1.refs_0_), channel_id=1, source_target_pairs={{0,1},{1,0},{2,3},{3,2},{4,5},{5,4},{6,7},{7,6},{8,9},{9,8},{10,11... | collective-permute-start | bytes 393224 | tf_op jit(solution)/shard_map/ppermute | solution.py:299
  17.0 5.8 %collective-permute-start.4 = (bf16[64,512]{1,0:T(8,128)(2,1)S(1)}, bf16[64,512]{1,0:T(8,128)(2,1)S(1)}, u32[]{:S(2)}, u32[]{:S(2)}) collective-permute-start(bf16[64,512]{1,0:T(8,128)(2,1)S(1)} %near_tests.1.near_ref), channel_id=1, source_target_pairs={{0,4},{1,5},{2,6},{3,7},{4,0},{5,1},{6,2},{7,3},{8,12},{9,13},{10,... | collective-permute-start | bytes 196616 | tf_op jit(solution)/shard_map/ppermute | solution.py:299
  19.9 6.4 %collective-permute-start.7 = (bf16[64,512]{1,0:T(8,128)(2,1)S(1)}, bf16[64,512]{1,0:T(8,128)(2,1)S(1)}, u32[]{:S(2)}, u32[]{:S(2)}) collective-permute-start(bf16[64,512]{1,0:T(8,128)(2,1)S(1)} %near_tests.1.near_ref), channel_id=1, source_target_pairs={{0,16},{8,24},{16,0},{24,8},{1,17},{9,25},{17,1},{25,9},{2,18},{10... | collective-permute-start | bytes 196616 | tf_op jit(solution)/shard_map/ppermute | solution.py:299
  22.8 4.4 %collective-permute-start.8 = (bf16[64,512]{1,0:T(8,128)(2,1)S(1)}, bf16[64,512]{1,0:T(8,128)(2,1)S(1)}, u32[]{:S(2)}, u32[]{:S(2)}) collective-permute-start(bf16[64,512]{1,0:T(8,128)(2,1)S(1)} %collective-permute-done.4.far_ref), channel_id=1, source_target_pairs={{0,16},{8,24},{16,0},{24,8},{1,17},{9,25},{17,1},{25,9},{2,18},{10... | collective-permute-start | bytes 196616 | tf_op jit(solution)/shard_map/ppermute | solution.py:299
  25.2 3.7 %collective-permute-start.12 = (f32[2,1024]{1,0:T(2,128)S(1)}, f32[2,1024]{1,0:T(2,128)S(1)}, u32[]{:S(2)}, u32[]{:S(2)}) collective-permute-start(f32[2,1024]{1,0:T(2,128)S(1)} %get-tuple-element.22), channel_id=1, source_target_pairs={{0,16},{8,24},{16,0},{24,8},{1,17},{9,25},{17,1},{25,9},{2,18},{10... | collective-permute-start | bytes 24584 | tf_op jit(solution)/shard_map/ppermute | solution.py:299
  26.3 2.8 %collective-permute-start.6 = (bf16[128,512]{1,0:T(8,128)(2,1)S(1)}, bf16[128,512]{1,0:T(8,128)(2,1)S(1)}, u32[]{:S(2)}, u32[]{:S(2)}) collective-permute-start(bf16[128,512]{1,0:T(8,128)(2,1)S(1)} %all_tests.2.refs_0_), channel_id=1, source_target_pairs={{0,8},{8,0},{16,24},{24,16},{1,9},{9,1},{17,25},{25,17},{2,10},{10... | collective-permute-start | bytes 393224 | tf_op jit(solution)/shard_map/ppermute | solution.py:299
  27.2 2.3 %collective-permute-start.9 = (bf16[128,512]{1,0:T(8,128)(2,1)S(1)}, bf16[128,512]{1,0:T(8,128)(2,1)S(1)}, u32[]{:S(2)}, u32[]{:S(2)}) collective-permute-start(bf16[128,512]{1,0:T(8,128)(2,1)S(1)} %all_tests.3.refs_0_), channel_id=1, source_target_pairs={{0,8},{8,0},{16,24},{24,16},{1,9},{9,1},{17,25},{25,17},{2,10},{10... | collective-permute-start | bytes 393224 | tf_op jit(solution)/shard_map/ppermute | solution.py:299
  29.0 1.2 %collective-permute-start.13 = (f32[1,1024]{1,0:T(1,128)S(1)}, f32[1,1024]{1,0:T(1,128)S(1)}, u32[]{:S(2)}, u32[]{:S(2)}) collective-permute-start(f32[1,1024]{1,0:T(1,128)S(1)} %slice_add_fusion), channel_id=1, source_target_pairs={{0,8},{8,0},{16,24},{24,16},{1,9},{9,1},{17,25},{25,17},{2,10},{10... | collective-permute-start | bytes 12296 | tf_op jit(solution)/shard_map/ppermute | solution.py:299
